TPU v7x, 128 devices: a whole 4x4x4 slice. The times are simulated.
128 devices in a mesh: row: 16 (over z, x_lo, core), col: 8 (over x_hi, y).
Axes of the slice: x: 4 (x_hi: 2, x_lo: 2; x = x_hi * 2 + x_lo), y: 4, z: 4, core: 2. Of those that a mesh axis runs over, the one named last changes fastest.
Arguments:
- pair: bfloat16 [512, 512, 128], P('row', 'col'), may hold values from -30 to 30
- in_gain: float32 [2, 128], replicated, may hold values from 0.5 to 1.5
- proj_weight: bfloat16 [2, 128, 512], replicated, may hold values from -0.5 to 0.5
- gate_weight: bfloat16 [2, 128, 128], replicated, may hold values from -0.5 to 0.5
- out_gain: float32 [2, 128], replicated, may hold values from 0.5 to 1.5
- out_weight: bfloat16 [2, 128, 128], replicated, may hold values from -0.5 to 0.5
Outputs:
- after_outgoing: bfloat16 [512, 512, 128], P('row', 'col')
- after_incoming: bfloat16 [512, 512, 128], P('row', 'col')
All inputs are finite; a program needn't handle non-finite values.
Results may differ from a plain program's by a relative error of at most 0.007.
Values may be sent and summed in bfloat16 or wider, within the bound.
A program may use at most 64 MiB of HBM per device.

v0:
```python
import jax
import jax.numpy as jnp
from jax import lax
from jax.sharding import PartitionSpec as P

EPS = 1e-05


def layer_norm(values, gain):
    values = values.astype(jnp.float32)
    average = jnp.mean(values, axis=-1, keepdims=True)
    centered = values - average
    variance = jnp.mean(centered * centered, axis=-1, keepdims=True)
    return centered * lax.rsqrt(variance + EPS) * gain


def to_channels(left_side, right_side):
    rows, cols, hidden = left_side.shape
    n_row = lax.axis_size("row")
    n_col = lax.axis_size("col")
    left_flip = jnp.transpose(left_side, (2, 0, 1))
    right_flip = jnp.transpose(right_side, (2, 0, 1))
    moved = (
        lax.all_to_all(
            left_flip.reshape(hidden, 1, rows, cols),
            ("row", "col"),
            split_axis=0,
            concat_axis=1,
            tiled=True,
        ),
        lax.all_to_all(
            right_flip.reshape(hidden, 1, rows, cols),
            ("row", "col"),
            split_axis=0,
            concat_axis=1,
            tiled=True,
        ),
    )

    def arrange(piece):
        channels = piece.shape[0]
        piece = piece.reshape(channels, n_row, n_col, rows, cols)
        return jnp.transpose(piece, (0, 1, 3, 2, 4)).reshape(channels, n_row * rows, n_col * cols)

    return (arrange(moved[0]), arrange(moved[1]))


def to_pairs(triangle, rows, cols):
    channels = triangle.shape[0]
    n_row = lax.axis_size("row")
    n_col = lax.axis_size("col")
    grid = triangle.reshape(channels, n_row, rows, n_col, cols)
    grid = jnp.transpose(grid, (0, 1, 3, 2, 4)).reshape(channels, n_row * n_col, rows, cols)
    moved = lax.all_to_all(grid, ("row", "col"), split_axis=1, concat_axis=0, tiled=True)
    return jnp.transpose(moved.reshape(channels * n_row * n_col, rows, cols), (1, 2, 0))


def gated_half(normed, weights, hidden):
    projected = jnp.dot(normed, weights, preferred_element_type=jnp.float32)
    return (jax.nn.sigmoid(projected[..., 0:hidden]) * projected[..., hidden : 2 * hidden]).astype(
        jnp.bfloat16
    )


def local(pair, in_gain, proj_weight, gate_weight, out_gain, out_weight):
    rows, cols, width = pair.shape
    hidden = out_weight.shape[1]
    current = pair
    results = []
    for which in range(2):
        normed = layer_norm(current, in_gain[which]).astype(jnp.bfloat16)
        left_side = gated_half(normed, proj_weight[which][:, 0 : 2 * hidden], hidden)
        right_side = gated_half(normed, proj_weight[which][:, 2 * hidden : 4 * hidden], hidden)
        left_chan, right_chan = to_channels(left_side, right_side)
        if which == 0:
            product = jnp.einsum(
                "cik,cjk->cij", left_chan, right_chan, preferred_element_type=jnp.float32
            )
        else:
            product = jnp.einsum(
                "cki,ckj->cij", left_chan, right_chan, preferred_element_type=jnp.float32
            )
        triangle = to_pairs(product.astype(jnp.bfloat16), rows, cols)
        tnorm = layer_norm(triangle, out_gain[which]).astype(jnp.bfloat16)
        gating = jax.nn.sigmoid(
            jnp.dot(normed, gate_weight[which], preferred_element_type=jnp.float32)
        )
        change = gating * jnp.dot(tnorm, out_weight[which], preferred_element_type=jnp.float32)
        current = (current.astype(jnp.float32) + change).astype(jnp.bfloat16)
        results.append(current)
    return (results[0], results[1])


def solution(mesh):
    in_specs = (P("row", "col", None), P(), P(), P(), P(), P())
    out_specs = (P("row", "col", None), P("row", "col", None))
    return jax.shard_map(local, mesh=mesh, in_specs=in_specs, out_specs=out_specs, check_vma=False)
```

profile of v0, /device:TPU:1, one launch (start us, length us, event | category | flops | bytes accessed | tf_op | source)
XLA Modules:
  0.0 147.2 jit_solution(16985735406872274105)
XLA Ops:
  0.6 1.4 convert_reduce_fusion.1
  2.0 1.7 %fusion.29 = f32[32,64]{1,0:T(8,128)S(1)} fusion(bf16[32,64,128]{2,1,0:T(8,128)(2,1)} %param.6, f32[32,64]{1,0:T(8,128)S(1)} %broadcast_multiply_fusion.3), kind=kLoop, calls=%fused_computation.43 | loop fusion | flops 1046528 | bytes 540672 | tf_op jit(solution)/shard_map/reduce_sum | solution.py:13
  3.7 0.8 slice_bitcast_fusion.11
  4.5 1.0 slice_bitcast_fusion
  5.5 1.8 %fusion.56 = f32[32,64,256]{2,1,0:T(8,128)S(1)} fusion(bf16[32,64,128]{2,1,0:T(8,128)(2,1)} %param.6, f32[128]{0:T(128)S(1)} %get-tuple-element.7, f32[32,64]{1,0:T(8,128)S(1)} %add_rsqrt_fusion.3, f32[32,64]{1,0:T(8,128)S(1)} %broadcast_multiply_fusion.3, bf16[128,512]{1,0:T(8,128)(2,1)S(1)} %get-tuple-element.3), kind=kOutput, calls=%fused_computation.79 | convolution fusion | flops 135528448 | bytes 2720256 | tf_op jit(solution)/shard_map/dot_general | solution.py:59
  7.6 1.6 %copy.22 = bf16[128,1,32,64]{3,2,1,0:T(8,128)(2,1)S(1)} copy(bf16[128,1,32,64]{0,3,2,1:T(8,128)(2,1)S(1)} %fusion.50) | data formatting | bytes 1048576 | tf_op jit(solution)/shard_map/reshape | solution.py:25
  9.2 1.4 reshape.174
  10.6 11.5 %all-to-all-start = ((bf16[128,2,1024]{2,1,0:T(2,128)(2,1)}), bf16[128,2,1024]{2,1,0:T(2,128)(2,1)S(1)}, u32[]{:S(2)}, u32[]{:S(2)}) async-start(bf16[128,2,1024]{2,1,0:T(2,128)(2,1)} %reshape.174), calls=%async_computation | async-start | bytes 1048576 | tf_op jit(solution)/shard_map/all_to_all | solution.py:24
  22.1 0.7 fusion.54
  23.1 1.6 %copy.24 = bf16[128,1,32,64]{3,2,1,0:T(8,128)(2,1)S(1)} copy(bf16[128,1,32,64]{0,3,2,1:T(8,128)(2,1)S(1)} %fusion.51) | data formatting | bytes 1048576 | tf_op jit(solution)/shard_map/reshape | solution.py:32
  24.7 1.4 reshape.176
  26.1 9.6 %all-to-all-done = bf16[128,2,1024]{2,1,0:T(2,128)(2,1)S(1)} async-done(((bf16[128,2,1024]{2,1,0:T(2,128)(2,1)}), bf16[128,2,1024]{2,1,0:T(2,128)(2,1)S(1)}, u32[]{:S(2)}, u32[]{:S(2)}) %all-to-all-start) | async-done | bytes 524320 | tf_op jit(solution)/shard_map/all_to_all | solution.py:24
  35.7 5.1 %all-to-all-start.1 = ((bf16[128,2,1024]{2,1,0:T(2,128)(2,1)}), bf16[128,2,1024]{2,1,0:T(2,128)(2,1)}, u32[]{:S(2)}, u32[]{:S(2)}) async-start(bf16[128,2,1024]{2,1,0:T(2,128)(2,1)} %reshape.176), calls=%async_computation.1 | async-start | bytes 1048576 | tf_op jit(solution)/shard_map/all_to_all | solution.py:31
  40.8 0.6 reshape.175
  41.9 0.6 reshape.150
  42.5 11.8 %all-to-all-done.1 = bf16[128,2,1024]{2,1,0:T(2,128)(2,1)} async-done(((bf16[128,2,1024]{2,1,0:T(2,128)(2,1)}), bf16[128,2,1024]{2,1,0:T(2,128)(2,1)}, u32[]{:S(2)}, u32[]{:S(2)}) %all-to-all-start.1) | async-done | bytes 524320 | tf_op jit(solution)/shard_map/all_to_all | solution.py:31
  54.2 2.3 %reshape.177 = bf16[128,1,32,64]{3,2,1,0:T(8,128)(2,1)S(1)} reshape(bf16[128,2,1024]{2,1,0:T(2,128)(2,1)} %all-to-all-done.1) | data formatting | bytes 1048576
  57.0 0.6 reshape.153
  57.6 0.5 convolution_convert_fusion.1
  58.0 0.5 reshape.154
  58.9 1.4 reshape.178
  60.2 4.4 %all-to-all-start.2 = ((bf16[128,2,1024]{2,1,0:T(2,128)(2,1)}), bf16[128,2,1024]{2,1,0:T(2,128)(2,1)S(1)}, u32[]{:S(2)}, u32[]{:S(2)}) async-start(bf16[128,2,1024]{2,1,0:T(2,128)(2,1)} %reshape.178), calls=%async_computation.2 | async-start | bytes 1048576 | tf_op jit(solution)/shard_map/all_to_all | solution.py:54
  64.7 0.7 fusion.17
  65.5 12.9 %all-to-all-done.2 = bf16[128,2,1024]{2,1,0:T(2,128)(2,1)S(1)} async-done(((bf16[128,2,1024]{2,1,0:T(2,128)(2,1)}), bf16[128,2,1024]{2,1,0:T(2,128)(2,1)S(1)}, u32[]{:S(2)}, u32[]{:S(2)}) %all-to-all-start.2) | async-done | bytes 524320 | tf_op jit(solution)/shard_map/all_to_all | solution.py:54
  78.3 0.6 reshape.179
  80.0 0.8 convert_reduce_fusion
  80.8 0.6 fusion.26
  81.5 0.7 fusion.59
  82.5 1.6 %copy.31 = bf16[128,1,32,64]{3,2,1,0:T(8,128)(2,1)S(1)} copy(bf16[128,1,32,64]{0,3,2,1:T(8,128)(2,1)S(1)} %fusion.53) | data formatting | bytes 1048576 | tf_op jit(solution)/shard_map/reshape | solution.py:32
  84.1 1.4 reshape.182
  85.5 4.4 %all-to-all-start.4 = ((bf16[128,2,1024]{2,1,0:T(2,128)(2,1)}), bf16[128,2,1024]{2,1,0:T(2,128)(2,1)S(1)}, u32[]{:S(2)}, u32[]{:S(2)}) async-start(bf16[128,2,1024]{2,1,0:T(2,128)(2,1)} %reshape.182), calls=%async_computation.4 | async-start | bytes 1048576 | tf_op jit(solution)/shard_map/all_to_all | solution.py:31
  89.9 0.7 fusion.61
  91.0 1.6 %copy.29 = bf16[128,1,32,64]{3,2,1,0:T(8,128)(2,1)S(1)} copy(bf16[128,1,32,64]{0,3,2,1:T(8,128)(2,1)S(1)} %fusion.52) | data formatting | bytes 1048576 | tf_op jit(solution)/shard_map/reshape | solution.py:25
  92.6 1.4 reshape.180
  94.0 9.6 %all-to-all-done.4 = bf16[128,2,1024]{2,1,0:T(2,128)(2,1)S(1)} async-done(((bf16[128,2,1024]{2,1,0:T(2,128)(2,1)}), bf16[128,2,1024]{2,1,0:T(2,128)(2,1)S(1)}, u32[]{:S(2)}, u32[]{:S(2)}) %all-to-all-start.4) | async-done | bytes 524320 | tf_op jit(solution)/shard_map/all_to_all | solution.py:31
  103.6 4.4 %all-to-all-start.3 = ((bf16[128,2,1024]{2,1,0:T(2,128)(2,1)}), bf16[128,2,1024]{2,1,0:T(2,128)(2,1)S(1)}, u32[]{:S(2)}, u32[]{:S(2)}) async-start(bf16[128,2,1024]{2,1,0:T(2,128)(2,1)} %reshape.180), calls=%async_computation.3 | async-start | bytes 1048576 | tf_op jit(solution)/shard_map/all_to_all | solution.py:24
  108.1 0.6 reshape.183
  109.1 1.4 reshape.161
  110.5 11.2 %all-to-all-done.3 = bf16[128,2,1024]{2,1,0:T(2,128)(2,1)S(1)} async-done(((bf16[128,2,1024]{2,1,0:T(2,128)(2,1)}), bf16[128,2,1024]{2,1,0:T(2,128)(2,1)S(1)}, u32[]{:S(2)}, u32[]{:S(2)}) %all-to-all-start.3) | async-done | bytes 524320 | tf_op jit(solution)/shard_map/all_to_all | solution.py:24
  121.7 0.6 reshape.181
  122.8 0.6 reshape.158
  123.9 0.5 reshape.162
  124.7 1.4 reshape.184
  126.1 4.4 %all-to-all-start.5 = ((bf16[128,2,1024]{2,1,0:T(2,128)(2,1)}), bf16[128,2,1024]{2,1,0:T(2,128)(2,1)S(1)}, u32[]{:S(2)}, u32[]{:S(2)}) async-start(bf16[128,2,1024]{2,1,0:T(2,128)(2,1)} %reshape.184), calls=%async_computation.5 | async-start | bytes 1048576 | tf_op jit(solution)/shard_map/all_to_all | solution.py:54
  130.5 0.7 fusion.19
  131.3 12.9 %all-to-all-done.5 = bf16[128,2,1024]{2,1,0:T(2,128)(2,1)S(1)} async-done(((bf16[128,2,1024]{2,1,0:T(2,128)(2,1)}), bf16[128,2,1024]{2,1,0:T(2,128)(2,1)S(1)}, u32[]{:S(2)}, u32[]{:S(2)}) %all-to-all-start.5) | async-done | bytes 524320 | tf_op jit(solution)/shard_map/all_to_all | solution.py:54
  144.2 0.6 reshape.185
  145.8 1.4 fusion.21
  (38 shorter events, 6.0 us)
Async XLA Ops:
  7.5 14.5 %copy-start.1 = (bf16[32,64,128]{2,1,0:T(8,128)(2,1)S(1)}, bf16[32,64,128]{2,1,0:T(8,128)(2,1)}, u32[]{:S(2)}) copy-start(bf16[32,64,128]{2,1,0:T(8,128)(2,1)} %param.6) | copy-start | bytes 1572868
  10.6 25.2 %all-to-all-start = ((bf16[128,2,1024]{2,1,0:T(2,128)(2,1)}), bf16[128,2,1024]{2,1,0:T(2,128)(2,1)S(1)}, u32[]{:S(2)}, u32[]{:S(2)}) async-start(bf16[128,2,1024]{2,1,0:T(2,128)(2,1)} %reshape.174), calls=%async_computation | async-start | bytes 1048576 | tf_op jit(solution)/shard_map/all_to_all | solution.py:24
  35.7 18.5 %all-to-all-start.1 = ((bf16[128,2,1024]{2,1,0:T(2,128)(2,1)}), bf16[128,2,1024]{2,1,0:T(2,128)(2,1)}, u32[]{:S(2)}, u32[]{:S(2)}) async-start(bf16[128,2,1024]{2,1,0:T(2,128)(2,1)} %reshape.176), calls=%async_computation.1 | async-start | bytes 1048576 | tf_op jit(solution)/shard_map/all_to_all | solution.py:31
  58.6 6.1 %copy-start.4 = (f32[2,128]{1,0:T(2,128)S(1)}, f32[2,128]{1,0:T(2,128)}, u32[]{:S(2)}) copy-start(f32[2,128]{1,0:T(2,128)} %param.10) | copy-start | bytes 3076
  58.6 6.1 %copy-start.5 = (bf16[2,128,128]{2,1,0:T(8,128)(2,1)S(1)}, bf16[2,128,128]{2,1,0:T(8,128)(2,1)}, u32[]{:S(2)}) copy-start(bf16[2,128,128]{2,1,0:T(8,128)(2,1)} %param.9) | copy-start | bytes 196612
  60.2 18.1 %all-to-all-start.2 = ((bf16[128,2,1024]{2,1,0:T(2,128)(2,1)}), bf16[128,2,1024]{2,1,0:T(2,128)(2,1)S(1)}, u32[]{:S(2)}, u32[]{:S(2)}) async-start(bf16[128,2,1024]{2,1,0:T(2,128)(2,1)} %reshape.178), calls=%async_computation.2 | async-start | bytes 1048576 | tf_op jit(solution)/shard_map/all_to_all | solution.py:54
  79.0 1.1 copy-start.3
  80.8 65.0 %copy-start = (bf16[32,64,128]{2,1,0:T(8,128)(2,1)}, bf16[32,64,128]{2,1,0:T(8,128)(2,1)S(1)}, u32[]{:S(2)}) copy-start(bf16[32,64,128]{2,1,0:T(8,128)(2,1)S(1)} %get-tuple-element.9) | copy-start | bytes 1572868
  85.5 18.1 %all-to-all-start.4 = ((bf16[128,2,1024]{2,1,0:T(2,128)(2,1)}), bf16[128,2,1024]{2,1,0:T(2,128)(2,1)S(1)}, u32[]{:S(2)}, u32[]{:S(2)}) async-start(bf16[128,2,1024]{2,1,0:T(2,128)(2,1)} %reshape.182), calls=%async_computation.4 | async-start | bytes 1048576 | tf_op jit(solution)/shard_map/all_to_all | solution.py:31
  103.6 18.1 %all-to-all-start.3 = ((bf16[128,2,1024]{2,1,0:T(2,128)(2,1)}), bf16[128,2,1024]{2,1,0:T(2,128)(2,1)S(1)}, u32[]{:S(2)}, u32[]{:S(2)}) async-start(bf16[128,2,1024]{2,1,0:T(2,128)(2,1)} %reshape.180), calls=%async_computation.3 | async-start | bytes 1048576 | tf_op jit(solution)/shard_map/all_to_all | solution.py:24
  122.3 1.1 copy-start.2
  126.1 18.1 %all-to-all-start.5 = ((bf16[128,2,1024]{2,1,0:T(2,128)(2,1)}), bf16[128,2,1024]{2,1,0:T(2,128)(2,1)S(1)}, u32[]{:S(2)}, u32[]{:S(2)}) async-start(bf16[128,2,1024]{2,1,0:T(2,128)(2,1)} %reshape.184), calls=%async_computation.5 | async-start | bytes 1048576 | tf_op jit(solution)/shard_map/all_to_all | solution.py:54
where the time goes:
time: 148 us; the launch traced here: 147 us
  waiting for transfers between devices  68 us (46%)
  starting transfers between devices  34.3 us (23%)
  local copies, waits for them, and re-layouts  28.4 us (19%)
  matrix products  8.5 us (6%)
  other arithmetic  6.94 us (5%)
    all_to_all x2, waiting for transfers between devices, to_pairs(): lax.all_to_all(grid, ('row', 'col'), split_axis=1, concat_axis=0, tiled=T...  25.8 us
    all_to_all x2, waiting for transfers between devices, to_channels(): lax.all_to_all(right_flip.reshape(hidden, 1, rows, cols), ('row', 'col'),...  21.4 us
    all_to_all x2, waiting for transfers between devices, to_channels(): lax.all_to_all(left_flip.reshape(hidden, 1, rows, cols), ('row', 'col'),...  20.8 us
    all_to_all x2, starting transfers between devices, to_channels(): lax.all_to_all(left_flip.reshape(hidden, 1, rows, cols), ('row', 'col'),...  15.9 us
    unnamed x24, local copies, waits for them, and re-layouts  13.6 us
    all_to_all x2, starting transfers between devices, to_channels(): lax.all_to_all(right_flip.reshape(hidden, 1, rows, cols), ('row', 'col'),...  9.48 us
    all_to_all x2, starting transfers between devices, to_pairs(): lax.all_to_all(grid, ('row', 'col'), split_axis=1, concat_axis=0, tiled=T...  8.87 us
    dot_general x4, matrix products, gated_half(): projected = jnp.dot(normed, weights, preferred_element_type=jnp.float32)  3.97 us
  transfers between devices with their start and end apart: 6, of which 6 were waited for; matrix products, arithmetic and copies ran while one was open for 9% of the time, Pallas kernels for 0%

commit v1 on v0

v1 whole, which is shorter than its diff:
```python
import jax
import jax.numpy as jnp
from jax import lax
from jax.experimental import pallas as pl
from jax.experimental.pallas import tpu as pltpu
from jax.sharding import PartitionSpec as P

EPS = 1e-05
MESH = pl.DeviceIdType.MESH
F32 = jnp.float32
BF16 = jnp.bfloat16
NT = (((1,), (1,)), ((), ()))
TN = (((0,), (0,)), ((), ()))


def norm_rows(values, gain):
    centered = values - jnp.mean(values, axis=0, keepdims=True)
    variance = jnp.mean(centered * centered, axis=0, keepdims=True)
    return (centered * lax.rsqrt(variance + EPS) * gain).astype(BF16)


def sigmoid(values):
    return 0.5 * jnp.tanh(0.5 * values) + 0.5


def swap_halves(first, second):
    return (
        jnp.concatenate([first[:, :64], second[:, :64]], axis=1),
        jnp.concatenate([first[:, 64:], second[:, 64:]], axis=1),
    )


def kernel(
    pair,
    in_gain,
    proj_weight,
    gate_weight,
    out_gain,
    out_weight,
    out0,
    out1,
    eye,
    proj_t,
    gate_t,
    outw_t,
    gains,
    zt,
    normed,
    flat_l,
    flat_r,
    send,
    recv,
    left,
    right,
    tsend,
    trecv,
    send_sem,
    recv_sem,
    tsend_sem,
    trecv_sem,
):
    row, col = lax.axis_index("row"), lax.axis_index("col")
    mine = row * 8 + col

    def peer(step):
        dr, dc = step // 8, lax.rem(step, 8)
        z = lax.rem(row // 4 + dr // 4, 4)
        lo = jnp.bitwise_xor(lax.rem(row, 4), lax.rem(dr, 4))
        hi = jnp.bitwise_xor(col // 4, dc // 4)
        y = lax.rem(lax.rem(col, 4) + lax.rem(dc, 4), 4)
        return z * 4 + lo, hi * 4 + y

    barrier = pltpu.get_barrier_semaphore()

    def greet(step, carry):
        pl.semaphore_signal(barrier, inc=1, device_id=peer(step), device_id_type=MESH)
        return carry

    lax.fori_loop(1, 128, greet, 0, unroll=8)

    ident = (
        lax.broadcasted_iota(jnp.int32, (128, 128), 0)
        == lax.broadcasted_iota(jnp.int32, (128, 128), 1)
    ).astype(F32)
    eye[...] = ident.astype(BF16)

    def flip(block):
        return lax.dot_general(eye[...], block, NT, preferred_element_type=F32)

    for u in range(2):
        for b in range(4):
            proj_t[u, 128 * b : 128 * (b + 1), :] = flip(
                proj_weight[u, :, 128 * b : 128 * (b + 1)]
            ).astype(BF16)
        gate_t[u] = flip(gate_weight[u]).astype(BF16)
        outw_t[u] = flip(out_weight[u]).astype(BF16)
        gains[0, u] = jnp.transpose(jnp.broadcast_to(in_gain[u : u + 1, :], (128, 128)))
        gains[1, u] = jnp.transpose(jnp.broadcast_to(out_gain[u : u + 1, :], (128, 128)))

    def project(u, q, zq):
        zt[q] = zq
        nq = norm_rows(zq, gains[0, u])
        normed[q] = nq
        proj = jnp.dot(proj_t[u], nq, preferred_element_type=F32)
        flat_l[pl.ds(q, 128, stride=16), :] = sigmoid(proj[0:128]) * proj[128:256]
        flat_r[pl.ds(q, 128, stride=16), :] = sigmoid(proj[256:384]) * proj[384:512]

    def first(q, carry):
        block = jnp.concatenate([pair[q], pair[q + 16]], axis=0)
        project(0, q, flip(block))
        return carry

    lax.fori_loop(0, 16, first, 0)
    pl.semaphore_wait(barrier, 127)

    for u in range(2):

        def pack(d):
            rows = pl.ds(pl.multiple_of(d * 16, 16), 16)
            send[u, d, 0] = flat_l[rows, :].astype(BF16)
            send[u, d, 1] = flat_r[rows, :].astype(BF16)

        def out_lr(step, carry):
            tr, tc = peer(step)
            d = tr * 8 + tc
            pack(d)
            pltpu.make_async_remote_copy(
                src_ref=send.at[u, d],
                dst_ref=recv.at[u, mine],
                send_sem=send_sem.at[u],
                recv_sem=recv_sem.at[u],
                device_id=(tr, tc),
                device_id_type=MESH,
            ).start()
            return carry

        lax.fori_loop(1, 128, out_lr, 0, unroll=2)
        pack(mine)
        recv[u, mine] = send[u, mine]
        pltpu.make_async_copy(
            recv.at[u, pl.ds(0, 127)], recv.at[u, pl.ds(0, 127)], recv_sem.at[u]
        ).wait()

        def arrange(r, carry):
            at = pl.multiple_of(r * 32, 32)
            for side, whole in enumerate((left, right)):
                for m in range(4):
                    lo, hi = swap_halves(recv[u, r * 8 + 2 * m, side], recv[u, r * 8 + 2 * m + 1, side])
                    whole[pl.ds(at, 16), 128 * m : 128 * (m + 1)] = lo
                    whole[pl.ds(at + 16, 16), 128 * m : 128 * (m + 1)] = hi
            return carry

        lax.fori_loop(0, 16, arrange, 0)

        for b in range(4):
            if u == 0:
                tri = lax.dot_general(
                    left[128 * b : 128 * (b + 1), :], right[...], NT, preferred_element_type=F32
                ).astype(BF16)
            else:
                tri = lax.dot_general(
                    left[:, 128 * b : 128 * (b + 1)], right[...], TN, preferred_element_type=F32
                ).astype(BF16)
            for rr in range(4):
                for m in range(4):
                    lo, hi = swap_halves(
                        tri[32 * rr : 32 * rr + 16, 128 * m : 128 * (m + 1)],
                        tri[32 * rr + 16 : 32 * rr + 32, 128 * m : 128 * (m + 1)],
                    )
                    tsend[u, (4 * b + rr) * 8 + 2 * m] = lo
                    tsend[u, (4 * b + rr) * 8 + 2 * m + 1] = hi

        def out_t(step, carry):
            tr, tc = peer(step)
            pltpu.make_async_remote_copy(
                src_ref=tsend.at[u, tr * 8 + tc],
                dst_ref=trecv.at[u, mine],
                send_sem=tsend_sem.at[u],
                recv_sem=trecv_sem.at[u],
                device_id=(tr, tc),
                device_id_type=MESH,
            ).start()
            return carry

        lax.fori_loop(1, 128, out_t, 0, unroll=8)
        trecv[u, mine] = tsend[u, mine]
        pltpu.make_async_copy(
            trecv.at[u, pl.ds(0, 127)], trecv.at[u, pl.ds(0, 127)], trecv_sem.at[u]
        ).wait()

        def widen(h, carry):
            flat_l[pl.ds(pl.multiple_of(h * 64, 64), 64), :] = (
                trecv[u, pl.ds(h * 4, 4)].astype(F32).reshape(64, 128)
            )
            return carry

        lax.fori_loop(0, 32, widen, 0, unroll=4)

        def finish(q, carry):
            tn = norm_rows(flat_l[pl.ds(q, 128, stride=16), :], gains[1, u])
            gate = sigmoid(jnp.dot(gate_t[u], normed[q], preferred_element_type=F32))
            change = gate * jnp.dot(outw_t[u], tn, preferred_element_type=F32)
            new = (zt[q] + change).astype(BF16)
            flipped = flip(new).astype(BF16)
            target = (out0, out1)[u]
            target[q] = flipped[:64]
            target[q + 16] = flipped[64:]
            zt[q] = new.astype(F32)
            return carry

        lax.fori_loop(0, 16, finish, 0)
        if u == 0:

            def again(q, carry):
                project(1, q, zt[q])
                return carry

            lax.fori_loop(0, 16, again, 0)

    for u in range(2):
        pltpu.make_async_copy(
            send.at[u, pl.ds(0, 127)], send.at[u, pl.ds(0, 127)], send_sem.at[u]
        ).wait()
        pltpu.make_async_copy(
            tsend.at[u, pl.ds(0, 127)], tsend.at[u, pl.ds(0, 127)], tsend_sem.at[u]
        ).wait()


def local(pair, in_gain, proj_weight, gate_weight, out_gain, out_weight):
    vmem = pl.BlockSpec(memory_space=pltpu.VMEM)
    shape = jax.ShapeDtypeStruct(pair.shape, BF16)
    return pl.pallas_call(
        kernel,
        out_shape=(shape, shape),
        in_specs=[vmem] * 6,
        out_specs=(vmem, vmem),
        scratch_shapes=[
            pltpu.VMEM((128, 128), BF16),
            pltpu.VMEM((2, 512, 128), BF16),
            pltpu.VMEM((2, 128, 128), BF16),
            pltpu.VMEM((2, 128, 128), BF16),
            pltpu.VMEM((2, 2, 128, 128), F32),
            pltpu.VMEM((16, 128, 128), F32),
            pltpu.VMEM((16, 128, 128), BF16),
            pltpu.VMEM((2048, 128), F32),
            pltpu.VMEM((2048, 128), F32),
            pltpu.VMEM((2, 128, 2, 16, 128), BF16),
            pltpu.VMEM((2, 128, 2, 16, 128), BF16),
            pltpu.VMEM((512, 512), BF16),
            pltpu.VMEM((512, 512), BF16),
            pltpu.VMEM((2, 128, 16, 128), BF16),
            pltpu.VMEM((2, 128, 16, 128), BF16),
            pltpu.SemaphoreType.DMA((2,)),
            pltpu.SemaphoreType.DMA((2,)),
            pltpu.SemaphoreType.DMA((2,)),
            pltpu.SemaphoreType.DMA((2,)),
        ],
        compiler_params=pltpu.CompilerParams(
            collective_id=0, has_side_effects=True, vmem_limit_bytes=40 << 20
        ),
        name="triangle",
    )(pair, in_gain, proj_weight, gate_weight, out_gain, out_weight)


def solution(mesh):
    in_specs = (P("row", "col", None), P(), P(), P(), P(), P())
    out_specs = (P("row", "col", None), P("row", "col", None))
    return jax.shard_map(local, mesh=mesh, in_specs=in_specs, out_specs=out_specs, check_vma=False)
```

time: 148 us -> 102 us (0.69)
  Pallas kernels: 0 us -> 94.7 us
  waiting for transfers between devices: 68 us -> 0 us
  starting transfers between devices: 34.3 us -> 0 us
  local copies, waits for them, and re-layouts: 28.4 us -> 6.61 us
  matrix products: 8.5 us -> 0 us
  other arithmetic: 6.94 us -> 0 us
    pallas_call x0 -> x1, Pallas kernels: none -> 94.7 us  [local(): pl.pallas_call(kernel, out_shape=(shape, shape), in_specs=[vmem] * 6, out...]
    all_to_all x6 -> x0, waiting for transfers between devices: 68 us -> none  [the longest x2 25.8 us: to_pairs(): lax.all_to_all(grid, ('row', 'col'), split_axis=1, concat_axis=0, tiled=T...]
    all_to_all x6 -> x0, starting transfers between devices: 34.3 us -> none  [the longest x2 15.9 us: to_channels(): lax.all_to_all(left_flip.reshape(hidden, 1, rows, cols), ('row', 'col'),...]
    dot_general x10 -> x0, matrix products: 8.5 us -> none  [the longest x4 3.97 us: gated_half(): projected = jnp.dot(normed, weights, preferred_element_type=jnp.float32)]
    reshape x8 -> x0, local copies, waits for them, and re-layouts: 8.04 us -> none  [the longest x2 3.24 us: to_channels(): left_flip.reshape(hidden, 1, rows, cols)]
    unnamed x24 -> x14, local copies, waits for them, and re-layouts: 13.6 us -> 6.61 us
    reduce_sum x7 -> x0, other arithmetic: 5 us -> none  [the longest x4 3.09 us: layer_norm(): variance = jnp.mean(centered * centered, axis=-1, keepdims=True)]
    another operation x4 -> x0, local copies, waits for them, and re-layouts: 3.23 us -> none
  transfers between devices with their start and end apart: 6 -> 0, of which waited for: 6 -> 0; matrix products, arithmetic and copies ran while one was open for 9% -> 0% of each run, Pallas kernels for 0% -> 0%
where the time goes in v1:
time: 102 us
  Pallas kernels  94.7 us (93%)
  local copies, waits for them, and re-layouts  6.61 us (6%)
    pallas_call x1, Pallas kernels, local(): pl.pallas_call(kernel, out_shape=(shape, shape), in_specs=[vmem] * 6, out...  94.7 us
    unnamed x14, local copies, waits for them, and re-layouts  6.61 us

profile of v1, /device:TPU:1, one launch (start us, length us, event | category | flops | bytes accessed | tf_op | source)
XLA Modules:
  0.0 102.0 jit_solution(8064217091413765242)
XLA Ops:
  0.6 0.0 copy-start
  0.6 1.0 %copy-done = bf16[32,64,128]{2,1,0:T(8,128)(2,1)S(1)} copy-done((bf16[32,64,128]{2,1,0:T(8,128)(2,1)S(1)}, bf16[32,64,128]{2,1,0:T(8,128)(2,1)}, u32[]{:S(2)}) %copy-start) | copy-done | bytes 524312
  1.7 0.0 copy-start.1
  1.7 0.9 copy-done.1
  2.6 0.0 copy-start.2
  2.6 0.8 copy-done.2
  3.5 0.0 copy-start.3
  3.5 0.8 copy-done.3
  4.3 0.0 copy-start.4
  4.3 0.7 copy-done.4
  5.0 0.0 copy-start.5
  5.0 0.7 copy-done.5
  5.7 94.7 %triangle.1 = (bf16[32,64,128]{2,1,0:T(8,128)(2,1)S(1)}, bf16[32,64,128]{2,1,0:T(8,128)(2,1)S(1)}) custom-call(bf16[32,64,128]{2,1,0:T(8,128)(2,1)S(1)} %copy-done, f32[2,128]{1,0:T(2,128)S(1)} %copy-done.4, bf16[2,128,512]{2,1,0:T(8,128)(2,1)S(1)} %copy-done.1, bf16[2,128,128]{2,1,0:T(8,128)(2,1)S(1)} %copy-done.2, f32[2,128]{1,0:T(2,128)S(1)} %copy-done.5, ...), custom_call_target="tpu_custom_call" | custom-call | tf_op jit(solution)/shard_map/triangle/pallas_call | solution.py:232
  100.4 0.8 copy.10
  101.2 0.8 copy.11
Async XLA Ops:
  0.6 1.0 %copy-start = (bf16[32,64,128]{2,1,0:T(8,128)(2,1)S(1)}, bf16[32,64,128]{2,1,0:T(8,128)(2,1)}, u32[]{:S(2)}) copy-start(bf16[32,64,128]{2,1,0:T(8,128)(2,1)} %pair.1) | copy-start | bytes 1572868
  1.7 0.9 copy-start.1
  2.6 0.8 copy-start.2
  3.5 0.8 copy-start.3
  4.3 0.7 copy-start.4
  5.0 0.7 copy-start.5

commit v2 on v1

v2 whole, which is shorter than its diff:
```python
import jax
import jax.numpy as jnp
from jax import lax
from jax.experimental import pallas as pl
from jax.experimental.pallas import tpu as pltpu
from jax.sharding import PartitionSpec as P

EPS = 1e-05
MESH = pl.DeviceIdType.MESH
F32 = jnp.float32
BF16 = jnp.bfloat16
TN = (((0,), (0,)), ((), ()))


def norm_rows(values, gain):
    centered = values - jnp.mean(values, axis=0, keepdims=True)
    variance = jnp.mean(centered * centered, axis=0, keepdims=True)
    return (centered * lax.rsqrt(variance + EPS) * gain).astype(BF16)


def sigmoid(values):
    return 0.5 * jnp.tanh(0.5 * values) + 0.5


def swap_halves(first, second):
    return (
        jnp.concatenate([first[:, :64], second[:, :64]], axis=1),
        jnp.concatenate([first[:, 64:], second[:, 64:]], axis=1),
    )


def kernel(
    pair_hbm,
    in_gain_hbm,
    proj_hbm,
    gate_hbm,
    out_gain_hbm,
    outw_hbm,
    out0,
    out1,
    pair,
    proj_w,
    gate_w,
    outw_w,
    in_gain,
    out_gain,
    proj_t,
    gate_t,
    outw_t,
    gains,
    zt,
    normed,
    flat_l,
    flat_r,
    flat_t,
    send_l,
    send_r,
    recv_l,
    recv_r,
    block0,
    block1,
    right,
    right_t,
    tsend,
    trecv,
    load_sem,
    send_sem,
    recv_r_sem,
    recv_l_sem,
    recv_t_sem,
):
    row, col = lax.axis_index("row"), lax.axis_index("col")
    mine = row * 8 + col
    outs = (out0, out1)

    def peer(step):
        dr, dc = step // 8, lax.rem(step, 8)
        z = lax.rem(row // 4 + dr // 4, 4)
        lo = jnp.bitwise_xor(lax.rem(row, 4), lax.rem(dr, 4))
        hi = jnp.bitwise_xor(col // 4, dc // 4)
        y = lax.rem(lax.rem(col, 4) + lax.rem(dc, 4), 4)
        return z * 4 + lo, hi * 4 + y

    def peer_of_pair(step):
        g, t = step // 32, lax.rem(step, 32)
        dr, parity = t // 2, lax.rem(t, 2)
        z = lax.rem(row // 4 + dr // 4, 4)
        lo = jnp.bitwise_xor(lax.rem(row, 4), lax.rem(dr, 4))
        return z * 4 + lo, jnp.bitwise_xor(col, 2 * g + parity)

    barrier = pltpu.get_barrier_semaphore()

    def greet(step, carry):
        pl.semaphore_signal(barrier, inc=1, device_id=peer(step), device_id_type=MESH)
        return carry

    lax.fori_loop(1, 128, greet, 0, unroll=8)

    loads = [
        pltpu.make_async_copy(src, dst, load_sem.at[i])
        for i, (src, dst) in enumerate(
            (
                (pair_hbm, pair),
                (proj_hbm, proj_w),
                (gate_hbm, gate_w),
                (outw_hbm, outw_w),
                (in_gain_hbm, in_gain),
                (out_gain_hbm, out_gain),
            )
        )
    ]
    for load in loads:
        load.start()
    for load in loads[1:]:
        load.wait()
    for u in range(2):
        for i, gain in enumerate((in_gain, out_gain)):
            flipped = jnp.transpose(jnp.broadcast_to(gain[u : u + 1, :], (128, 128)))
            gains[i, u] = jnp.concatenate([flipped, flipped], axis=1)
        proj_t[u] = jnp.transpose(proj_w[u])
        gate_t[u] = jnp.transpose(gate_w[u])
        outw_t[u] = jnp.transpose(outw_w[u])
    loads[0].wait()

    def project(u, q, side, flat):
        proj = jnp.dot(
            proj_t[u, 256 * side : 256 * side + 256, :], normed[q], preferred_element_type=F32
        )
        gated = sigmoid(proj[:128]) * proj[128:]
        for k in range(2):
            flat[pl.ds(2 * q + k, 128, stride=16), :] = gated[:, 128 * k : 128 * (k + 1)]

    def first(q, carry):
        block = jnp.concatenate(
            [pair[2 * q], pair[2 * q + 16], pair[2 * q + 1], pair[2 * q + 17]], axis=0
        )
        zq = jnp.transpose(block).astype(F32)
        zt[q] = zq
        normed[q] = norm_rows(zq, gains[0, 0])
        project(0, q, 1, flat_r)
        project(0, q, 0, flat_l)
        return carry

    lax.fori_loop(0, 8, first, 0, unroll=4)
    pl.semaphore_wait(barrier, 127)

    def send_side(u, flat, send, recv, sem_of, lo, hi, to):
        def one(step, carry):
            tr, tc = to(step)
            d = tr * 8 + tc
            send[u, d] = flat[pl.ds(pl.multiple_of(d * 16, 16), 16), :].astype(BF16)
            pltpu.make_async_remote_copy(
                src_ref=send.at[u, d],
                dst_ref=recv.at[u, mine],
                send_sem=send_sem.at[u],
                recv_sem=sem_of,
                device_id=(tr, tc),
                device_id_type=MESH,
            ).start()
            return carry

        lax.fori_loop(lo, hi, one, 0, unroll=4)

    def wait_tiles(ref, sem, count):
        pltpu.make_async_copy(ref.at[pl.ds(0, count)], ref.at[pl.ds(0, count)], sem).wait()

    def own(u, flat, recv):
        recv[u, mine] = flat[pl.ds(pl.multiple_of(mine * 16, 16), 16), :].astype(BF16)

    for u in range(2):
        to_left = peer if u == 0 else peer_of_pair
        send_side(u, flat_r, send_r, recv_r, recv_r_sem.at[u], 1, 128, peer)
        own(u, flat_r, recv_r)
        if u == 1:

            def late_left(q, carry):
                project(1, q, 0, flat_l)
                return carry

            lax.fori_loop(0, 8, late_left, 0, unroll=4)
        for g in range(4):
            send_side(
                u, flat_l, send_l, recv_l, recv_l_sem.at[u, g], max(32 * g, 1), 32 * g + 32, to_left
            )
        own(u, flat_l, recv_l)
        if u == 1:

            def write_first(q, carry):
                flipped = jnp.transpose(zt[q].astype(BF16))
                for k in range(2):
                    out0[2 * q + k] = flipped[128 * k : 128 * k + 64]
                    out0[2 * q + k + 16] = flipped[128 * k + 64 : 128 * k + 128]
                return carry

            lax.fori_loop(0, 8, write_first, 0, unroll=2)

        wait_tiles(recv_r.at[u], recv_r_sem.at[u], 127)

        def arrange(r, carry):
            at = pl.multiple_of(r * 32, 32)
            for m in range(4):
                lo, hi = swap_halves(recv_r[u, r * 8 + 2 * m], recv_r[u, r * 8 + 2 * m + 1])
                right[pl.ds(at, 16), 128 * m : 128 * (m + 1)] = lo
                right[pl.ds(at + 16, 16), 128 * m : 128 * (m + 1)] = hi
            return carry

        lax.fori_loop(0, 16, arrange, 0, unroll=4)
        if u == 0:
            right_t[...] = jnp.transpose(right[...])

        for g in range(4):
            wait_tiles(recv_l.at[u], recv_l_sem.at[u, g], 31 if g == 0 else 32)
            if u == 0:
                part = lax.rem(row // 4 + (4 - g), 4)
                for rr in range(4):
                    for m in range(4):
                        at = (part * 4 + rr) * 8 + 2 * m
                        lo, hi = swap_halves(recv_l[u, at], recv_l[u, at + 1])
                        block0[32 * rr : 32 * rr + 16, 128 * m : 128 * (m + 1)] = lo
                        block0[32 * rr + 16 : 32 * rr + 32, 128 * m : 128 * (m + 1)] = hi
                tri = jnp.dot(block0[...], right_t[...], preferred_element_type=F32).astype(BF16)
            else:
                part = jnp.bitwise_xor(col // 2, g)
                for r in range(16):
                    at = r * 8 + 2 * part
                    lo, hi = swap_halves(recv_l[u, at], recv_l[u, at + 1])
                    block1[32 * r : 32 * r + 16, :] = lo
                    block1[32 * r + 16 : 32 * r + 32, :] = hi
                tri = lax.dot_general(
                    block1[...], right[...], TN, preferred_element_type=F32
                ).astype(BF16)
            for rr in range(4):
                for m in range(4):
                    lo, hi = swap_halves(
                        tri[32 * rr : 32 * rr + 16, 128 * m : 128 * (m + 1)],
                        tri[32 * rr + 16 : 32 * rr + 32, 128 * m : 128 * (m + 1)],
                    )
                    tsend[u, (part * 4 + rr) * 8 + 2 * m] = lo
                    tsend[u, (part * 4 + rr) * 8 + 2 * m + 1] = hi

            def home(t, carry):
                tr = part * 4 + jnp.bitwise_xor(lax.rem(row, 4), t // 8)
                tc = jnp.bitwise_xor(col, lax.rem(t, 8))

                @pl.when(jnp.logical_or(tr != row, tc != col))
                def _():
                    pltpu.make_async_remote_copy(
                        src_ref=tsend.at[u, tr * 8 + tc],
                        dst_ref=trecv.at[u, mine],
                        send_sem=send_sem.at[u],
                        recv_sem=recv_t_sem.at[u],
                        device_id=(tr, tc),
                        device_id_type=MESH,
                    ).start()

                return carry

            lax.fori_loop(0, 32, home, 0, unroll=4)
        trecv[u, mine] = tsend[u, mine]
        wait_tiles(trecv.at[u], recv_t_sem.at[u], 127)

        def widen(h, carry):
            flat_t[pl.ds(pl.multiple_of(h * 64, 64), 64), :] = (
                trecv[u, pl.ds(h * 4, 4)].astype(F32).reshape(64, 128)
            )
            return carry

        lax.fori_loop(0, 32, widen, 0, unroll=4)

        def finish(q, carry):
            tri_q = jnp.concatenate(
                [flat_t[pl.ds(2 * q + k, 128, stride=16), :] for k in range(2)], axis=1
            )
            tn = norm_rows(tri_q, gains[1, u])
            gate = sigmoid(jnp.dot(gate_t[u], normed[q], preferred_element_type=F32))
            change = gate * jnp.dot(outw_t[u], tn, preferred_element_type=F32)
            new = (zt[q] + change).astype(BF16)
            if u == 0:
                zq = new.astype(F32)
                zt[q] = zq
                normed[q] = norm_rows(zq, gains[0, 1])
                project(1, q, 1, flat_r)
            else:
                flipped = jnp.transpose(new)
                for k in range(2):
                    out1[2 * q + k] = flipped[128 * k : 128 * k + 64]
                    out1[2 * q + k + 16] = flipped[128 * k + 64 : 128 * k + 128]
            return carry

        lax.fori_loop(0, 8, finish, 0, unroll=4)

    for u in range(2):
        for _ in range(3):
            wait_tiles(send_r.at[u], send_sem.at[u], 127)


def local(pair, in_gain, proj_weight, gate_weight, out_gain, out_weight):
    vmem = pl.BlockSpec(memory_space=pltpu.VMEM)
    hbm = pl.BlockSpec(memory_space=pltpu.HBM)
    shape = jax.ShapeDtypeStruct(pair.shape, BF16)
    tiles = pltpu.VMEM((2, 128, 16, 128), BF16)
    dma = pltpu.SemaphoreType.DMA
    return pl.pallas_call(
        kernel,
        out_shape=(shape, shape),
        in_specs=[hbm] * 6,
        out_specs=(vmem, vmem),
        scratch_shapes=[
            pltpu.VMEM((32, 64, 128), BF16),
            pltpu.VMEM((2, 128, 512), BF16),
            pltpu.VMEM((2, 128, 128), BF16),
            pltpu.VMEM((2, 128, 128), BF16),
            pltpu.VMEM((2, 128), F32),
            pltpu.VMEM((2, 128), F32),
            pltpu.VMEM((2, 512, 128), BF16),
            pltpu.VMEM((2, 128, 128), BF16),
            pltpu.VMEM((2, 128, 128), BF16),
            pltpu.VMEM((2, 2, 128, 256), F32),
            pltpu.VMEM((8, 128, 256), F32),
            pltpu.VMEM((8, 128, 256), BF16),
            pltpu.VMEM((2048, 128), F32),
            pltpu.VMEM((2048, 128), F32),
            pltpu.VMEM((2048, 128), F32),
            tiles,
            tiles,
            tiles,
            tiles,
            pltpu.VMEM((128, 512), BF16),
            pltpu.VMEM((512, 128), BF16),
            pltpu.VMEM((512, 512), BF16),
            pltpu.VMEM((512, 512), BF16),
            tiles,
            tiles,
            dma((6,)),
            dma((2,)),
            dma((2,)),
            dma((2, 4)),
            dma((2,)),
        ],
        compiler_params=pltpu.CompilerParams(
            collective_id=0, has_side_effects=True, vmem_limit_bytes=60 << 20
        ),
        name="triangle",
    )(pair, in_gain, proj_weight, gate_weight, out_gain, out_weight)


def solution(mesh):
    in_specs = (P("row", "col", None), P(), P(), P(), P(), P())
    out_specs = (P("row", "col", None), P("row", "col", None))
    return jax.shard_map(local, mesh=mesh, in_specs=in_specs, out_specs=out_specs, check_vma=False)
```

time: 102 us -> 72.4 us (0.71)
  Pallas kernels: 94.7 us -> 68.9 us
  local copies, waits for them, and re-layouts: 6.61 us -> 2.72 us
    pallas_call x1, Pallas kernels: 94.7 us -> 68.9 us  [local(): pl.pallas_call(kernel, out_shape=(shape, shape), in_specs=[hbm] * 6, out_...]
    unnamed x14 -> x4, local copies, waits for them, and re-layouts: 6.61 us -> 2.72 us
where the time goes in v2:
time: 72.4 us; the launch traced here: 72.3 us
  Pallas kernels  68.9 us (95%)
  local copies, waits for them, and re-layouts  2.72 us (4%)
    pallas_call x1, Pallas kernels, local(): pl.pallas_call(kernel, out_shape=(shape, shape), in_specs=[hbm] * 6, out_...  68.9 us
    unnamed x4, local copies, waits for them, and re-layouts  2.72 us

profile of v2, /device:TPU:1, one launch (start us, length us, event | category | flops | bytes accessed | tf_op | source)
XLA Modules:
  0.0 72.3 jit_solution(11146026779283771937)
XLA Ops:
  0.6 68.9 %triangle.1 = (bf16[32,64,128]{2,1,0:T(8,128)(2,1)}, bf16[32,64,128]{2,1,0:T(8,128)(2,1)}) custom-call(bf16[32,64,128]{2,1,0:T(8,128)(2,1)} %pair_hbm.1, f32[2,128]{1,0:T(2,128)} %in_gain_hbm.1, bf16[2,128,512]{2,1,0:T(8,128)(2,1)} %proj_hbm.1, bf16[2,128,128]{2,1,0:T(8,128)(2,1)} %gate_hbm.1, f32[2,128]{1,0:T(2,128)} %out_gain_hbm.1, ...), custom_call_target="tpu_custom_call" | custom-call | tf_op jit(solution)/shard_map/triangle/pallas_call | solution.py:303
  69.6 0.0 copy-start
  69.6 1.9 %copy.10 = bf16[32,64,128]{2,1,0:T(8,128)(2,1)} copy(bf16[32,64,128]{2,1,0:T(8,128)(2,1)} %get-tuple-element.4) | data formatting | bytes 1048576
  71.5 0.0 copy-done
  71.5 0.8 %copy.11 = bf16[32,64,128]{2,1,0:T(8,128)(2,1)} copy(bf16[32,64,128]{2,1,0:T(8,128)(2,1)S(1)} %copy-done) | data formatting | bytes 1048576
Async XLA Ops:
  69.6 1.9 %copy-start = (bf16[32,64,128]{2,1,0:T(8,128)(2,1)S(1)}, bf16[32,64,128]{2,1,0:T(8,128)(2,1)}, u32[]{:S(2)}) copy-start(bf16[32,64,128]{2,1,0:T(8,128)(2,1)} %get-tuple-element.5) | copy-start | bytes 1572868

commit v3 on v2

--- a/solution.py
+++ b/solution.py
@@ -9,6 +9,8 @@
 MESH = pl.DeviceIdType.MESH
 F32 = jnp.float32
 BF16 = jnp.bfloat16
+FARTHEST = (-1698185745, 19170134)
+PLANES = (2, 1, 3, 0)
 TN = (((0,), (0,)), ((), ()))
 
 
@@ -73,28 +75,44 @@
     mine = row * 8 + col
     outs = (out0, out1)
 
-    def peer(step):
-        dr, dc = step // 8, lax.rem(step, 8)
-        z = lax.rem(row // 4 + dr // 4, 4)
-        lo = jnp.bitwise_xor(lax.rem(row, 4), lax.rem(dr, 4))
-        hi = jnp.bitwise_xor(col // 4, dc // 4)
-        y = lax.rem(lax.rem(col, 4) + lax.rem(dc, 4), 4)
-        return z * 4 + lo, hi * 4 + y
-
-    def peer_of_pair(step):
-        g, t = step // 32, lax.rem(step, 32)
-        dr, parity = t // 2, lax.rem(t, 2)
-        z = lax.rem(row // 4 + dr // 4, 4)
-        lo = jnp.bitwise_xor(lax.rem(row, 4), lax.rem(dr, 4))
-        return z * 4 + lo, jnp.bitwise_xor(col, 2 * g + parity)
+    z = row // 4
+
+    def mod4(value):
+        return jnp.bitwise_and(value, 3)
+
+    def visit(zs, skip_self, act):
+        def both_cores(j, word):
+            code = jnp.bitwise_and(lax.shift_right_logical(jnp.int32(word), 4 * j), 15)
+            dx, dy = code // 4, mod4(code)
+            dx = jnp.bitwise_xor(dx, dx // 2)
+            dy = jnp.bitwise_xor(dy, dy // 2)
+            tc = jnp.bitwise_xor(col // 4, dx // 2) * 4 + mod4(col + dy)
+            tr = zs * 4 + jnp.bitwise_xor(mod4(row), lax.rem(dx, 2) * 2)
+            act(jnp.bitwise_xor(tr, 1), tc)
+            if skip_self:
+
+                @pl.when(jnp.logical_or(tr != row, tc != col))
+                def _():
+                    act(tr, tc)
+
+            else:
+                act(tr, tc)
+
+        for word in FARTHEST:
+
+            def one(j, carry):
+                both_cores(j, word)
+                return carry
+
+            lax.fori_loop(0, 8, one, 0, unroll=2)
 
     barrier = pltpu.get_barrier_semaphore()
 
-    def greet(step, carry):
-        pl.semaphore_signal(barrier, inc=1, device_id=peer(step), device_id_type=MESH)
-        return carry
-
-    lax.fori_loop(1, 128, greet, 0, unroll=8)
+    def greet(tr, tc):
+        pl.semaphore_signal(barrier, inc=1, device_id=(tr, tc), device_id_type=MESH)
+
+    for dz in PLANES:
+        visit(mod4(z + dz), dz == 0, greet)
 
     loads = [
         pltpu.make_async_copy(src, dst, load_sem.at[i])
@@ -144,9 +162,8 @@
     lax.fori_loop(0, 8, first, 0, unroll=4)
     pl.semaphore_wait(barrier, 127)
 
-    def send_side(u, flat, send, recv, sem_of, lo, hi, to):
-        def one(step, carry):
-            tr, tc = to(step)
+    def send_side(u, flat, send, recv, sem_of, zs, skip_self):
+        def one(tr, tc):
             d = tr * 8 + tc
             send[u, d] = flat[pl.ds(pl.multiple_of(d * 16, 16), 16), :].astype(BF16)
             pltpu.make_async_remote_copy(
@@ -157,9 +174,8 @@
                 device_id=(tr, tc),
                 device_id_type=MESH,
             ).start()
-            return carry
-
-        lax.fori_loop(lo, hi, one, 0, unroll=4)
+
+        visit(zs, skip_self, one)
 
     def wait_tiles(ref, sem, count):
         pltpu.make_async_copy(ref.at[pl.ds(0, count)], ref.at[pl.ds(0, count)], sem).wait()
@@ -168,8 +184,8 @@
         recv[u, mine] = flat[pl.ds(pl.multiple_of(mine * 16, 16), 16), :].astype(BF16)
 
     for u in range(2):
-        to_left = peer if u == 0 else peer_of_pair
-        send_side(u, flat_r, send_r, recv_r, recv_r_sem.at[u], 1, 128, peer)
+        for dz in PLANES:
+            send_side(u, flat_r, send_r, recv_r, recv_r_sem.at[u], mod4(z + dz), dz == 0)
         own(u, flat_r, recv_r)
         if u == 1:
 
@@ -178,10 +194,9 @@
                 return carry
 
             lax.fori_loop(0, 8, late_left, 0, unroll=4)
-        for g in range(4):
-            send_side(
-                u, flat_l, send_l, recv_l, recv_l_sem.at[u, g], max(32 * g, 1), 32 * g + 32, to_left
-            )
+        for g, dz in enumerate(PLANES):
+            zs = mod4((z if u == 0 else col // 2) + dz)
+            send_side(u, flat_l, send_l, recv_l, recv_l_sem.at[u, g], zs, u == 1 or dz == 0)
         own(u, flat_l, recv_l)
         if u == 1:
 
@@ -208,10 +223,22 @@
         if u == 0:
             right_t[...] = jnp.transpose(right[...])
 
-        for g in range(4):
-            wait_tiles(recv_l.at[u], recv_l_sem.at[u, g], 31 if g == 0 else 32)
+        for g, dz in enumerate(PLANES):
+            part = mod4(z + (4 - dz))
             if u == 0:
-                part = lax.rem(row // 4 + (4 - g), 4)
+                wait_tiles(recv_l.at[u], recv_l_sem.at[u, g], 31 if dz == 0 else 32)
+            else:
+                mixed = part == col // 2
+
+                @pl.when(mixed)
+                def _():
+                    wait_tiles(recv_l.at[u], recv_l_sem.at[u, g], 31)
+
+                @pl.when(jnp.logical_not(mixed))
+                def _():
+                    wait_tiles(recv_l.at[u], recv_l_sem.at[u, g], 32)
+
+            if u == 0:
                 for rr in range(4):
                     for m in range(4):
                         at = (part * 4 + rr) * 8 + 2 * m
@@ -220,7 +247,6 @@
                         block0[32 * rr + 16 : 32 * rr + 32, 128 * m : 128 * (m + 1)] = hi
                 tri = jnp.dot(block0[...], right_t[...], preferred_element_type=F32).astype(BF16)
             else:
-                part = jnp.bitwise_xor(col // 2, g)
                 for r in range(16):
                     at = r * 8 + 2 * part
                     lo, hi = swap_halves(recv_l[u, at], recv_l[u, at + 1])
@@ -238,24 +264,17 @@
                     tsend[u, (part * 4 + rr) * 8 + 2 * m] = lo
                     tsend[u, (part * 4 + rr) * 8 + 2 * m + 1] = hi
 
-            def home(t, carry):
-                tr = part * 4 + jnp.bitwise_xor(lax.rem(row, 4), t // 8)
-                tc = jnp.bitwise_xor(col, lax.rem(t, 8))
-
-                @pl.when(jnp.logical_or(tr != row, tc != col))
-                def _():
-                    pltpu.make_async_remote_copy(
-                        src_ref=tsend.at[u, tr * 8 + tc],
-                        dst_ref=trecv.at[u, mine],
-                        send_sem=send_sem.at[u],
-                        recv_sem=recv_t_sem.at[u],
-                        device_id=(tr, tc),
-                        device_id_type=MESH,
-                    ).start()
-
-                return carry
-
-            lax.fori_loop(0, 32, home, 0, unroll=4)
+            def home(tr, tc):
+                pltpu.make_async_remote_copy(
+                    src_ref=tsend.at[u, tr * 8 + tc],
+                    dst_ref=trecv.at[u, mine],
+                    send_sem=send_sem.at[u],
+                    recv_sem=recv_t_sem.at[u],
+                    device_id=(tr, tc),
+                    device_id_type=MESH,
+                ).start()
+
+            visit(part, dz == 0, home)
         trecv[u, mine] = tsend[u, mine]
         wait_tiles(trecv.at[u], recv_t_sem.at[u], 127)
 

time: 72.4 us -> 65.2 us (0.901)
  Pallas kernels: 68.9 us -> 61.7 us
    pallas_call x1, Pallas kernels: 68.9 us -> 61.7 us  [local(): pl.pallas_call(kernel, out_shape=(shape, shape), in_specs=[hbm] * 6, out_...]
where the time goes in v3:
time: 65.2 us; the launch traced here: 65.1 us
  Pallas kernels  61.7 us (95%)
  local copies, waits for them, and re-layouts  2.72 us (4%)
    pallas_call x1, Pallas kernels, local(): pl.pallas_call(kernel, out_shape=(shape, shape), in_specs=[hbm] * 6, out_...  61.7 us
    unnamed x4, local copies, waits for them, and re-layouts  2.72 us

profile of v3, /device:TPU:1, one launch (start us, length us, event | category | flops | bytes accessed | tf_op | source)
XLA Modules:
  0.0 65.1 jit_solution(4683105329788258685)
XLA Ops:
  0.6 61.7 %triangle.1 = (bf16[32,64,128]{2,1,0:T(8,128)(2,1)}, bf16[32,64,128]{2,1,0:T(8,128)(2,1)}) custom-call(bf16[32,64,128]{2,1,0:T(8,128)(2,1)} %pair_hbm.1, f32[2,128]{1,0:T(2,128)} %in_gain_hbm.1, bf16[2,128,512]{2,1,0:T(8,128)(2,1)} %proj_hbm.1, bf16[2,128,128]{2,1,0:T(8,128)(2,1)} %gate_hbm.1, f32[2,128]{1,0:T(2,128)} %out_gain_hbm.1, ...), custom_call_target="tpu_custom_call" | custom-call | tf_op jit(solution)/shard_map/triangle/pallas_call | solution.py:322
  62.4 0.0 copy-start
  62.4 1.9 %copy.10 = bf16[32,64,128]{2,1,0:T(8,128)(2,1)} copy(bf16[32,64,128]{2,1,0:T(8,128)(2,1)} %get-tuple-element.4) | data formatting | bytes 1048576
  64.3 0.0 copy-done
  64.3 0.8 %copy.11 = bf16[32,64,128]{2,1,0:T(8,128)(2,1)} copy(bf16[32,64,128]{2,1,0:T(8,128)(2,1)S(1)} %copy-done) | data formatting | bytes 1048576
Async XLA Ops:
  62.4 1.9 %copy-start = (bf16[32,64,128]{2,1,0:T(8,128)(2,1)S(1)}, bf16[32,64,128]{2,1,0:T(8,128)(2,1)}, u32[]{:S(2)}) copy-start(bf16[32,64,128]{2,1,0:T(8,128)(2,1)} %get-tuple-element.5) | copy-start | bytes 1572868

commit v4 on v3

--- a/solution.py
+++ b/solution.py
@@ -9,8 +9,9 @@
 MESH = pl.DeviceIdType.MESH
 F32 = jnp.float32
 BF16 = jnp.bfloat16
-FARTHEST = (-1698185745, 19170134)
-PLANES = (2, 1, 3, 0)
+FARTHEST = 0x3124756
+GROUPS = (((2, 1), (2, 0)), ((1, 1), (3, 0)), ((3, 1), (1, 0)), ((0, 1), (0, 0)))
+NT = (((1,), (1,)), ((), ()))
 TN = (((0,), (0,)), ((), ()))
 
 
@@ -29,6 +30,38 @@
         jnp.concatenate([first[:, :64], second[:, :64]], axis=1),
         jnp.concatenate([first[:, 64:], second[:, 64:]], axis=1),
     )
+
+
+def updated(q, flat_t, zt, normed, gain, gate_weight, out_weight):
+    tri_q = jnp.concatenate([flat_t[pl.ds(2 * q + k, 128, stride=16), :] for k in range(2)], axis=1)
+    tn = norm_rows(tri_q, gain)
+    gate = sigmoid(jnp.dot(gate_weight, normed[q], preferred_element_type=F32))
+    change = gate * jnp.dot(out_weight, tn, preferred_element_type=F32)
+    return (zt[q] + change).astype(BF16)
+
+
+def last_kernel(
+    first, zt, normed, flat_t, gate_t, outw_t, gain, out0, out1, second, first_sem, second_sem
+):
+    whole = pltpu.make_async_copy(first, out0, first_sem)
+    whole.start()
+
+    def part(q, k):
+        rows = pl.ds(2 * q + 16 * k, 2)
+        return pltpu.make_async_copy(second.at[rows], out1.at[rows], second_sem)
+
+    def finish(q, carry):
+        flipped = jnp.transpose(updated(q, flat_t, zt, normed, gain[...], gate_t[...], outw_t[...]))
+        for k in range(2):
+            second[2 * q + k] = flipped[128 * k : 128 * k + 64]
+            second[2 * q + k + 16] = flipped[128 * k + 64 : 128 * k + 128]
+        for k in range(2):
+            part(q, k).start()
+        return carry
+
+    lax.fori_loop(0, 8, finish, 0, unroll=4)
+    pltpu.make_async_copy(second, out1, second_sem).wait()
+    whole.wait()
 
 
 def kernel(
@@ -39,7 +72,12 @@
     out_gain_hbm,
     outw_hbm,
     out0,
-    out1,
+    zt,
+    normed,
+    flat_t,
+    gate_t1,
+    outw_t1,
+    gain1,
     pair,
     proj_w,
     gate_w,
@@ -50,11 +88,8 @@
     gate_t,
     outw_t,
     gains,
-    zt,
-    normed,
     flat_l,
     flat_r,
-    flat_t,
     send_l,
     send_r,
     recv_l,
@@ -62,7 +97,6 @@
     block0,
     block1,
     right,
-    right_t,
     tsend,
     trecv,
     load_sem,
@@ -73,46 +107,40 @@
 ):
     row, col = lax.axis_index("row"), lax.axis_index("col")
     mine = row * 8 + col
-    outs = (out0, out1)
 
     z = row // 4
 
     def mod4(value):
         return jnp.bitwise_and(value, 3)
 
-    def visit(zs, skip_self, act):
-        def both_cores(j, word):
-            code = jnp.bitwise_and(lax.shift_right_logical(jnp.int32(word), 4 * j), 15)
-            dx, dy = code // 4, mod4(code)
-            dx = jnp.bitwise_xor(dx, dx // 2)
-            dy = jnp.bitwise_xor(dy, dy // 2)
-            tc = jnp.bitwise_xor(col // 4, dx // 2) * 4 + mod4(col + dy)
-            tr = zs * 4 + jnp.bitwise_xor(mod4(row), lax.rem(dx, 2) * 2)
-            act(jnp.bitwise_xor(tr, 1), tc)
-            if skip_self:
-
-                @pl.when(jnp.logical_or(tr != row, tc != col))
-                def _():
-                    act(tr, tc)
-
-            else:
-                act(tr, tc)
-
-        for word in FARTHEST:
-
-            def one(j, carry):
-                both_cores(j, word)
-                return carry
-
-            lax.fori_loop(0, 8, one, 0, unroll=2)
+    def visit(group, act):
+        def step(j, carry):
+            code = jnp.bitwise_and(lax.shift_right_logical(jnp.int32(FARTHEST), 4 * j), 7)
+            tc = jnp.bitwise_xor(col // 4, code // 4) * 4 + mod4(col + code)
+            for zs, lo in group:
+                for e in range(2):
+                    tr = zs * 4 + lo * 2 + jnp.bitwise_xor(jnp.bitwise_and(row, 1), 1 - e)
+
+                    @pl.when(jnp.logical_or(tr != row, tc != col))
+                    def _():
+                        act(tr, tc)
+
+            return carry
+
+        lax.fori_loop(0, 8, step, 0, unroll=2)
+
+    def shifted(zs, lo, g):
+        return [(mod4(zs + dz), jnp.bitwise_xor(lo, dl)) for dz, dl in GROUPS[g]]
+
+    x_lo = lax.rem(row // 2, 2)
 
     barrier = pltpu.get_barrier_semaphore()
 
     def greet(tr, tc):
         pl.semaphore_signal(barrier, inc=1, device_id=(tr, tc), device_id_type=MESH)
 
-    for dz in PLANES:
-        visit(mod4(z + dz), dz == 0, greet)
+    for g in range(4):
+        visit(shifted(z, x_lo, g), greet)
 
     loads = [
         pltpu.make_async_copy(src, dst, load_sem.at[i])
@@ -138,6 +166,9 @@
         proj_t[u] = jnp.transpose(proj_w[u])
         gate_t[u] = jnp.transpose(gate_w[u])
         outw_t[u] = jnp.transpose(outw_w[u])
+    gate_t1[...] = gate_t[1]
+    outw_t1[...] = outw_t[1]
+    gain1[...] = gains[1, 1]
     loads[0].wait()
 
     def project(u, q, side, flat):
@@ -162,7 +193,7 @@
     lax.fori_loop(0, 8, first, 0, unroll=4)
     pl.semaphore_wait(barrier, 127)
 
-    def send_side(u, flat, send, recv, sem_of, zs, skip_self):
+    def send_side(u, flat, send, recv, sem_of, group):
         def one(tr, tc):
             d = tr * 8 + tc
             send[u, d] = flat[pl.ds(pl.multiple_of(d * 16, 16), 16), :].astype(BF16)
@@ -175,7 +206,7 @@
                 device_id_type=MESH,
             ).start()
 
-        visit(zs, skip_self, one)
+        visit(group, one)
 
     def wait_tiles(ref, sem, count):
         pltpu.make_async_copy(ref.at[pl.ds(0, count)], ref.at[pl.ds(0, count)], sem).wait()
@@ -184,8 +215,8 @@
         recv[u, mine] = flat[pl.ds(pl.multiple_of(mine * 16, 16), 16), :].astype(BF16)
 
     for u in range(2):
-        for dz in PLANES:
-            send_side(u, flat_r, send_r, recv_r, recv_r_sem.at[u], mod4(z + dz), dz == 0)
+        for g in range(4):
+            send_side(u, flat_r, send_r, recv_r, recv_r_sem.at[u], shifted(z, x_lo, g))
         own(u, flat_r, recv_r)
         if u == 1:
 
@@ -194,9 +225,9 @@
                 return carry
 
             lax.fori_loop(0, 8, late_left, 0, unroll=4)
-        for g, dz in enumerate(PLANES):
-            zs = mod4((z if u == 0 else col // 2) + dz)
-            send_side(u, flat_l, send_l, recv_l, recv_l_sem.at[u, g], zs, u == 1 or dz == 0)
+        for g in range(4):
+            base = (z, x_lo) if u == 0 else (col // 2, lax.rem(col, 2))
+            send_side(u, flat_l, send_l, recv_l, recv_l_sem.at[u, g], shifted(*base, g))
         own(u, flat_l, recv_l)
         if u == 1:
 
@@ -220,36 +251,34 @@
             return carry
 
         lax.fori_loop(0, 16, arrange, 0, unroll=4)
-        if u == 0:
-            right_t[...] = jnp.transpose(right[...])
-
-        for g, dz in enumerate(PLANES):
-            part = mod4(z + (4 - dz))
+
+        for g in range(4):
+            group = [(mod4(z + 4 - dz), jnp.bitwise_xor(x_lo, dl)) for dz, dl in GROUPS[g]]
+            rho = [zs * 2 + lo for zs, lo in group]
             if u == 0:
-                wait_tiles(recv_l.at[u], recv_l_sem.at[u, g], 31 if dz == 0 else 32)
-            else:
-                mixed = part == col // 2
-
-                @pl.when(mixed)
-                def _():
-                    wait_tiles(recv_l.at[u], recv_l_sem.at[u, g], 31)
-
-                @pl.when(jnp.logical_not(mixed))
-                def _():
-                    wait_tiles(recv_l.at[u], recv_l_sem.at[u, g], 32)
-
-            if u == 0:
+                wait_tiles(recv_l.at[u], recv_l_sem.at[u, g], 31 if (0, 0) in GROUPS[g] else 32)
                 for rr in range(4):
                     for m in range(4):
-                        at = (part * 4 + rr) * 8 + 2 * m
+                        at = (rho[rr // 2] * 2 + rr % 2) * 8 + 2 * m
                         lo, hi = swap_halves(recv_l[u, at], recv_l[u, at + 1])
                         block0[32 * rr : 32 * rr + 16, 128 * m : 128 * (m + 1)] = lo
                         block0[32 * rr + 16 : 32 * rr + 32, 128 * m : 128 * (m + 1)] = hi
-                tri = jnp.dot(block0[...], right_t[...], preferred_element_type=F32).astype(BF16)
+                tri = lax.dot_general(
+                    block0[...], right[...], NT, preferred_element_type=F32
+                ).astype(BF16)
             else:
+                with_own = jnp.logical_or(rho[0] == col, rho[1] == col)
+
+                @pl.when(with_own)
+                def _():
+                    wait_tiles(recv_l.at[u], recv_l_sem.at[u, g], 31)
+
+                @pl.when(jnp.logical_not(with_own))
+                def _():
+                    wait_tiles(recv_l.at[u], recv_l_sem.at[u, g], 32)
+
                 for r in range(16):
-                    at = r * 8 + 2 * part
-                    lo, hi = swap_halves(recv_l[u, at], recv_l[u, at + 1])
+                    lo, hi = swap_halves(recv_l[u, r * 8 + rho[0]], recv_l[u, r * 8 + rho[1]])
                     block1[32 * r : 32 * r + 16, :] = lo
                     block1[32 * r + 16 : 32 * r + 32, :] = hi
                 tri = lax.dot_general(
@@ -261,8 +290,9 @@
                         tri[32 * rr : 32 * rr + 16, 128 * m : 128 * (m + 1)],
                         tri[32 * rr + 16 : 32 * rr + 32, 128 * m : 128 * (m + 1)],
                     )
-                    tsend[u, (part * 4 + rr) * 8 + 2 * m] = lo
-                    tsend[u, (part * 4 + rr) * 8 + 2 * m + 1] = hi
+                    at = (rho[rr // 2] * 2 + rr % 2) * 8 + 2 * m
+                    tsend[u, at] = lo
+                    tsend[u, at + 1] = hi
 
             def home(tr, tc):
                 pltpu.make_async_remote_copy(
@@ -274,7 +304,7 @@
                     device_id_type=MESH,
                 ).start()
 
-            visit(part, dz == 0, home)
+            visit(group, home)
         trecv[u, mine] = tsend[u, mine]
         wait_tiles(trecv.at[u], recv_t_sem.at[u], 127)
 
@@ -286,27 +316,17 @@
 
         lax.fori_loop(0, 32, widen, 0, unroll=4)
 
-        def finish(q, carry):
-            tri_q = jnp.concatenate(
-                [flat_t[pl.ds(2 * q + k, 128, stride=16), :] for k in range(2)], axis=1
-            )
-            tn = norm_rows(tri_q, gains[1, u])
-            gate = sigmoid(jnp.dot(gate_t[u], normed[q], preferred_element_type=F32))
-            change = gate * jnp.dot(outw_t[u], tn, preferred_element_type=F32)
-            new = (zt[q] + change).astype(BF16)
-            if u == 0:
+        if u == 0:
+
+            def finish(q, carry):
+                new = updated(q, flat_t, zt, normed, gains[1, 0], gate_t[0], outw_t[0])
                 zq = new.astype(F32)
                 zt[q] = zq
                 normed[q] = norm_rows(zq, gains[0, 1])
                 project(1, q, 1, flat_r)
-            else:
-                flipped = jnp.transpose(new)
-                for k in range(2):
-                    out1[2 * q + k] = flipped[128 * k : 128 * k + 64]
-                    out1[2 * q + k + 16] = flipped[128 * k + 64 : 128 * k + 128]
-            return carry
-
-        lax.fori_loop(0, 8, finish, 0, unroll=4)
+                return carry
+
+            lax.fori_loop(0, 8, finish, 0, unroll=4)
 
     for u in range(2):
         for _ in range(3):
@@ -319,11 +339,23 @@
     shape = jax.ShapeDtypeStruct(pair.shape, BF16)
     tiles = pltpu.VMEM((2, 128, 16, 128), BF16)
     dma = pltpu.SemaphoreType.DMA
-    return pl.pallas_call(
+    operands = [
+        pltpu.with_memory_space_constraint(x, pltpu.HBM)
+        for x in (pair, in_gain, proj_weight, gate_weight, out_gain, out_weight)
+    ]
+    handed = pl.pallas_call(
         kernel,
-        out_shape=(shape, shape),
+        out_shape=(
+            shape,
+            jax.ShapeDtypeStruct((8, 128, 256), F32),
+            jax.ShapeDtypeStruct((8, 128, 256), BF16),
+            jax.ShapeDtypeStruct((2048, 128), F32),
+            jax.ShapeDtypeStruct((128, 128), BF16),
+            jax.ShapeDtypeStruct((128, 128), BF16),
+            jax.ShapeDtypeStruct((128, 256), F32),
+        ),
         in_specs=[hbm] * 6,
-        out_specs=(vmem, vmem),
+        out_specs=(vmem,) * 7,
         scratch_shapes=[
             pltpu.VMEM((32, 64, 128), BF16),
             pltpu.VMEM((2, 128, 512), BF16),
@@ -335,18 +367,14 @@
             pltpu.VMEM((2, 128, 128), BF16),
             pltpu.VMEM((2, 128, 128), BF16),
             pltpu.VMEM((2, 2, 128, 256), F32),
-            pltpu.VMEM((8, 128, 256), F32),
-            pltpu.VMEM((8, 128, 256), BF16),
             pltpu.VMEM((2048, 128), F32),
             pltpu.VMEM((2048, 128), F32),
-            pltpu.VMEM((2048, 128), F32),
             tiles,
             tiles,
             tiles,
             tiles,
             pltpu.VMEM((128, 512), BF16),
             pltpu.VMEM((512, 128), BF16),
-            pltpu.VMEM((512, 512), BF16),
             pltpu.VMEM((512, 512), BF16),
             tiles,
             tiles,
@@ -357,10 +385,19 @@
             dma((2,)),
         ],
         compiler_params=pltpu.CompilerParams(
-            collective_id=0, has_side_effects=True, vmem_limit_bytes=60 << 20
+            collective_id=0, has_side_effects=True, vmem_limit_bytes=24 << 20
         ),
         name="triangle",
-    )(pair, in_gain, proj_weight, gate_weight, out_gain, out_weight)
+    )(*operands)
+    return pl.pallas_call(
+        last_kernel,
+        out_shape=(shape, shape),
+        in_specs=[vmem] * 7,
+        out_specs=(hbm, hbm),
+        scratch_shapes=[pltpu.VMEM((32, 64, 128), BF16), dma, dma],
+        compiler_params=pltpu.CompilerParams(vmem_limit_bytes=16 << 20),
+        name="last",
+    )(*handed)
 
 
 def solution(mesh):

time: 65.2 us -> 61.6 us (0.945)
  local copies, waits for them, and re-layouts: 2.72 us -> 0 us
  Pallas kernels: 61.7 us -> 60.9 us
    unnamed x4 -> x0, local copies, waits for them, and re-layouts: 2.72 us -> none
    pallas_call x1 -> x2, Pallas kernels: 61.7 us -> 60.9 us  [the longest x1 59.1 us: local(): pl.pallas_call(kernel, out_shape=(shape, jax.ShapeDtypeStruct((8, 128, 25...]
where the time goes in v4:
time: 61.6 us; the launch traced here: 61.5 us
  Pallas kernels  60.9 us (99%)
  between operations  0.64 us (1%)
    pallas_call x1, Pallas kernels, local(): pl.pallas_call(kernel, out_shape=(shape, jax.ShapeDtypeStruct((8, 128, 25...  59.1 us
    pallas_call x1, Pallas kernels, local(): pl.pallas_call(last_kernel, out_shape=(shape, shape), in_specs=[vmem] * 7...  1.81 us

profile of v4, /device:TPU:1, one launch (start us, length us, event | category | flops | bytes accessed | tf_op | source)
XLA Modules:
  0.0 61.5 jit_solution(11769058115988057884)
XLA Ops:
  0.6 59.1 %triangle.1 = (bf16[32,64,128]{2,1,0:T(8,128)(2,1)S(1)}, f32[8,128,256]{2,1,0:T(8,128)S(1)}, bf16[8,128,256]{2,1,0:T(8,128)(2,1)S(1)}, f32[2048,128]{1,0:T(8,128...) custom-call(bf16[32,64,128]{2,1,0:T(8,128)(2,1)} %pair_hbm.1, ...), custom_call_target="tpu_custom_call" | custom-call | tf_op jit(solution)/shard_map/triangle/pallas_call | solution.py:346
  59.7 1.8 %last.1 = (bf16[32,64,128]{2,1,0:T(8,128)(2,1)}, bf16[32,64,128]{2,1,0:T(8,128)(2,1)}) custom-call(bf16[32,64,128]{2,1,0:T(8,128)(2,1)S(1)} %get-tuple-element.9.first, f32[8,128,256]{2,1,0:T(8,128)S(1)} %get-tuple-element.10.zt, bf16[8,128,256]{2,1,0:T(8,128)(2,1)S(1)} %get-tuple-element.11.normed, f32[2048,128]{1,0:T(8,128)S(1)} %get-tuple-element.12.flat_t, ...), custom_call_target="tpu_custom_call" | custom-call | tf_op jit(solution)/shard_map/last/pallas_call | solution.py:392

commit v5 on v4

--- a/solution.py
+++ b/solution.py
@@ -9,6 +9,7 @@
 MESH = pl.DeviceIdType.MESH
 F32 = jnp.float32
 BF16 = jnp.bfloat16
+UNROLL = 8
 FARTHEST = 0x3124756
 GROUPS = (((2, 1), (2, 0)), ((1, 1), (3, 0)), ((3, 1), (1, 0)), ((0, 1), (0, 0)))
 NT = (((1,), (1,)), ((), ()))
@@ -32,16 +33,15 @@
     )
 
 
-def updated(q, flat_t, zt, normed, gain, gate_weight, out_weight):
+def updated(q, flat_t, zt, gate, gain, out_weight):
     tri_q = jnp.concatenate([flat_t[pl.ds(2 * q + k, 128, stride=16), :] for k in range(2)], axis=1)
     tn = norm_rows(tri_q, gain)
-    gate = sigmoid(jnp.dot(gate_weight, normed[q], preferred_element_type=F32))
-    change = gate * jnp.dot(out_weight, tn, preferred_element_type=F32)
+    change = gate[q] * jnp.dot(out_weight, tn, preferred_element_type=F32)
     return (zt[q] + change).astype(BF16)
 
 
 def last_kernel(
-    first, zt, normed, flat_t, gate_t, outw_t, gain, out0, out1, second, first_sem, second_sem
+    first, zt, gate, flat_t, outw_t, gain, out0, out1, second, first_sem, second_sem
 ):
     whole = pltpu.make_async_copy(first, out0, first_sem)
     whole.start()
@@ -51,7 +51,7 @@
         return pltpu.make_async_copy(second.at[rows], out1.at[rows], second_sem)
 
     def finish(q, carry):
-        flipped = jnp.transpose(updated(q, flat_t, zt, normed, gain[...], gate_t[...], outw_t[...]))
+        flipped = jnp.transpose(updated(q, flat_t, zt, gate, gain[...], outw_t[...]))
         for k in range(2):
             second[2 * q + k] = flipped[128 * k : 128 * k + 64]
             second[2 * q + k + 16] = flipped[128 * k + 64 : 128 * k + 128]
@@ -73,9 +73,8 @@
     outw_hbm,
     out0,
     zt,
-    normed,
+    gate,
     flat_t,
-    gate_t1,
     outw_t1,
     gain1,
     pair,
@@ -88,6 +87,7 @@
     gate_t,
     outw_t,
     gains,
+    normed,
     flat_l,
     flat_r,
     send_l,
@@ -100,7 +100,9 @@
     tsend,
     trecv,
     load_sem,
-    send_sem,
+    send_r_sem,
+    send_l_sem,
+    send_t_sem,
     recv_r_sem,
     recv_l_sem,
     recv_t_sem,
@@ -113,34 +115,36 @@
     def mod4(value):
         return jnp.bitwise_and(value, 3)
 
-    def visit(group, act):
+    def visit(group, skip_self, act, core=None):
         def step(j, carry):
             code = jnp.bitwise_and(lax.shift_right_logical(jnp.int32(FARTHEST), 4 * j), 7)
             tc = jnp.bitwise_xor(col // 4, code // 4) * 4 + mod4(col + code)
             for zs, lo in group:
-                for e in range(2):
-                    tr = zs * 4 + lo * 2 + jnp.bitwise_xor(jnp.bitwise_and(row, 1), 1 - e)
-
-                    @pl.when(jnp.logical_or(tr != row, tc != col))
-                    def _():
+                for e in range(2) if core is None else (core,):
+                    tr = zs * 4 + lo * 2 + e
+
+                    if not skip_self:
                         act(tr, tc)
+                    else:
+
+                        @pl.when(jnp.logical_or(tr != row, tc != col))
+                        def _():
+                            act(tr, tc)
 
             return carry
 
-        lax.fori_loop(0, 8, step, 0, unroll=2)
+        lax.fori_loop(0, 8, step, 0, unroll=UNROLL)
 
     def shifted(zs, lo, g):
         return [(mod4(zs + dz), jnp.bitwise_xor(lo, dl)) for dz, dl in GROUPS[g]]
 
+    def back(g):
+        return [(mod4(z + 4 - dz), jnp.bitwise_xor(x_lo, dl)) for dz, dl in GROUPS[g]]
+
+    def has_own(g):
+        return (0, 0) in GROUPS[g]
+
     x_lo = lax.rem(row // 2, 2)
-
-    barrier = pltpu.get_barrier_semaphore()
-
-    def greet(tr, tc):
-        pl.semaphore_signal(barrier, inc=1, device_id=(tr, tc), device_id_type=MESH)
-
-    for g in range(4):
-        visit(shifted(z, x_lo, g), greet)
 
     loads = [
         pltpu.make_async_copy(src, dst, load_sem.at[i])
@@ -148,28 +152,31 @@
             (
                 (pair_hbm, pair),
                 (proj_hbm, proj_w),
+                (in_gain_hbm, in_gain),
                 (gate_hbm, gate_w),
                 (outw_hbm, outw_w),
-                (in_gain_hbm, in_gain),
                 (out_gain_hbm, out_gain),
             )
         )
     ]
     for load in loads:
         load.start()
-    for load in loads[1:]:
+    barrier = pltpu.get_barrier_semaphore()
+
+    def greet(tr, tc):
+        pl.semaphore_signal(barrier, inc=1, device_id=(tr, tc), device_id_type=MESH)
+
+    for g in range(4):
+        visit(shifted(z, x_lo, g), has_own(g), greet)
+
+    def prepare(u, i, gain):
+        flipped = jnp.transpose(jnp.broadcast_to(gain[u : u + 1, :], (128, 128)))
+        gains[i, u] = jnp.concatenate([flipped, flipped], axis=1)
+
+    for load in loads[:3]:
         load.wait()
-    for u in range(2):
-        for i, gain in enumerate((in_gain, out_gain)):
-            flipped = jnp.transpose(jnp.broadcast_to(gain[u : u + 1, :], (128, 128)))
-            gains[i, u] = jnp.concatenate([flipped, flipped], axis=1)
-        proj_t[u] = jnp.transpose(proj_w[u])
-        gate_t[u] = jnp.transpose(gate_w[u])
-        outw_t[u] = jnp.transpose(outw_w[u])
-    gate_t1[...] = gate_t[1]
-    outw_t1[...] = outw_t[1]
-    gain1[...] = gains[1, 1]
-    loads[0].wait()
+    prepare(0, 0, in_gain)
+    proj_t[0] = jnp.transpose(proj_w[0])
 
     def project(u, q, side, flat):
         proj = jnp.dot(
@@ -187,26 +194,25 @@
         zt[q] = zq
         normed[q] = norm_rows(zq, gains[0, 0])
         project(0, q, 1, flat_r)
-        project(0, q, 0, flat_l)
         return carry
 
     lax.fori_loop(0, 8, first, 0, unroll=4)
     pl.semaphore_wait(barrier, 127)
 
-    def send_side(u, flat, send, recv, sem_of, group):
+    def send_side(u, flat, send, recv, out_sem, in_sem, group, skip_self):
         def one(tr, tc):
             d = tr * 8 + tc
             send[u, d] = flat[pl.ds(pl.multiple_of(d * 16, 16), 16), :].astype(BF16)
             pltpu.make_async_remote_copy(
                 src_ref=send.at[u, d],
                 dst_ref=recv.at[u, mine],
-                send_sem=send_sem.at[u],
-                recv_sem=sem_of,
+                send_sem=out_sem,
+                recv_sem=in_sem,
                 device_id=(tr, tc),
                 device_id_type=MESH,
             ).start()
 
-        visit(group, one)
+        visit(group, skip_self, one)
 
     def wait_tiles(ref, sem, count):
         pltpu.make_async_copy(ref.at[pl.ds(0, count)], ref.at[pl.ds(0, count)], sem).wait()
@@ -214,21 +220,78 @@
     def own(u, flat, recv):
         recv[u, mine] = flat[pl.ds(pl.multiple_of(mine * 16, 16), 16), :].astype(BF16)
 
+    def wait_left(sem, ref, u, g, group, own_row, static_own):
+        if u == 0:
+            wait_tiles(ref.at[u], sem.at[u, g], 31 if static_own else 32)
+        else:
+            rho = [zs * 2 + lo for zs, lo in group]
+            with_own = jnp.logical_or(rho[0] == own_row, rho[1] == own_row)
+
+            @pl.when(with_own)
+            def _():
+                wait_tiles(ref.at[u], sem.at[u, g], 31)
+
+            @pl.when(jnp.logical_not(with_own))
+            def _():
+                wait_tiles(ref.at[u], sem.at[u, g], 32)
+
+    def left_base(u):
+        return (z, x_lo) if u == 0 else (col // 2, lax.rem(col, 2))
+
+    def sent_left(u, g):
+        wait_left(send_l_sem, send_l, u, g, shifted(*left_base(u), g), z * 2 + x_lo, has_own(g))
+
+    def sent_right(u):
+        wait_tiles(send_r.at[u], send_r_sem.at[u], 127)
+
     for u in range(2):
         for g in range(4):
-            send_side(u, flat_r, send_r, recv_r, recv_r_sem.at[u], shifted(z, x_lo, g))
+            send_side(
+                u,
+                flat_r,
+                send_r,
+                recv_r,
+                send_r_sem.at[u],
+                recv_r_sem.at[u],
+                shifted(z, x_lo, g),
+                has_own(g),
+            )
         own(u, flat_r, recv_r)
-        if u == 1:
-
-            def late_left(q, carry):
-                project(1, q, 0, flat_l)
-                return carry
-
-            lax.fori_loop(0, 8, late_left, 0, unroll=4)
+
+        def late_left(q, carry):
+            project(u, q, 0, flat_l)
+            return carry
+
+        lax.fori_loop(0, 8, late_left, 0, unroll=4)
         for g in range(4):
-            base = (z, x_lo) if u == 0 else (col // 2, lax.rem(col, 2))
-            send_side(u, flat_l, send_l, recv_l, recv_l_sem.at[u, g], shifted(*base, g))
+            send_side(
+                u,
+                flat_l,
+                send_l,
+                recv_l,
+                send_l_sem.at[u, g],
+                recv_l_sem.at[u, g],
+                shifted(*left_base(u), g),
+                u == 1 or has_own(g),
+            )
         own(u, flat_l, recv_l)
+        if u == 0:
+            for load in loads[3:]:
+                load.wait()
+            for v in range(2):
+                gate_t[v] = jnp.transpose(gate_w[v])
+                outw_t[v] = jnp.transpose(outw_w[v])
+                prepare(v, 1, out_gain)
+            prepare(1, 0, in_gain)
+            proj_t[1] = jnp.transpose(proj_w[1])
+            outw_t1[...] = outw_t[1]
+            gain1[...] = gains[1, 1]
+
+        def open_gate(q, carry):
+            gate[q] = sigmoid(jnp.dot(gate_t[u], normed[q], preferred_element_type=F32))
+            return carry
+
+        lax.fori_loop(0, 8, open_gate, 0, unroll=4)
         if u == 1:
 
             def write_first(q, carry):
@@ -252,11 +315,21 @@
 
         lax.fori_loop(0, 16, arrange, 0, unroll=4)
 
+        def home(tr, tc):
+            pltpu.make_async_remote_copy(
+                src_ref=tsend.at[u, tr * 8 + tc],
+                dst_ref=trecv.at[u, mine],
+                send_sem=send_t_sem.at[u],
+                recv_sem=recv_t_sem.at[u],
+                device_id=(tr, tc),
+                device_id_type=MESH,
+            ).start()
+
         for g in range(4):
-            group = [(mod4(z + 4 - dz), jnp.bitwise_xor(x_lo, dl)) for dz, dl in GROUPS[g]]
+            group = back(g)
             rho = [zs * 2 + lo for zs, lo in group]
+            wait_left(recv_l_sem, recv_l, u, g, group, col, has_own(g))
             if u == 0:
-                wait_tiles(recv_l.at[u], recv_l_sem.at[u, g], 31 if (0, 0) in GROUPS[g] else 32)
                 for rr in range(4):
                     for m in range(4):
                         at = (rho[rr // 2] * 2 + rr % 2) * 8 + 2 * m
@@ -267,16 +340,6 @@
                     block0[...], right[...], NT, preferred_element_type=F32
                 ).astype(BF16)
             else:
-                with_own = jnp.logical_or(rho[0] == col, rho[1] == col)
-
-                @pl.when(with_own)
-                def _():
-                    wait_tiles(recv_l.at[u], recv_l_sem.at[u, g], 31)
-
-                @pl.when(jnp.logical_not(with_own))
-                def _():
-                    wait_tiles(recv_l.at[u], recv_l_sem.at[u, g], 32)
-
                 for r in range(16):
                     lo, hi = swap_halves(recv_l[u, r * 8 + rho[0]], recv_l[u, r * 8 + rho[1]])
                     block1[32 * r : 32 * r + 16, :] = lo
@@ -294,17 +357,10 @@
                     tsend[u, at] = lo
                     tsend[u, at + 1] = hi
 
-            def home(tr, tc):
-                pltpu.make_async_remote_copy(
-                    src_ref=tsend.at[u, tr * 8 + tc],
-                    dst_ref=trecv.at[u, mine],
-                    send_sem=send_sem.at[u],
-                    recv_sem=recv_t_sem.at[u],
-                    device_id=(tr, tc),
-                    device_id_type=MESH,
-                ).start()
-
-            visit(group, home)
+            visit(group, has_own(g), home, 0 if u == 0 else None)
+        if u == 0:
+            for g in range(4):
+                visit(back(g), has_own(g), home, 1)
         trecv[u, mine] = tsend[u, mine]
         wait_tiles(trecv.at[u], recv_t_sem.at[u], 127)
 
@@ -319,7 +375,7 @@
         if u == 0:
 
             def finish(q, carry):
-                new = updated(q, flat_t, zt, normed, gains[1, 0], gate_t[0], outw_t[0])
+                new = updated(q, flat_t, zt, gate, gains[1, 0], outw_t[0])
                 zq = new.astype(F32)
                 zt[q] = zq
                 normed[q] = norm_rows(zq, gains[0, 1])
@@ -329,8 +385,10 @@
             lax.fori_loop(0, 8, finish, 0, unroll=4)
 
     for u in range(2):
-        for _ in range(3):
-            wait_tiles(send_r.at[u], send_sem.at[u], 127)
+        sent_right(u)
+        for g in range(4):
+            sent_left(u, g)
+        wait_tiles(tsend.at[u], send_t_sem.at[u], 127)
 
 
 def local(pair, in_gain, proj_weight, gate_weight, out_gain, out_weight):
@@ -348,14 +406,13 @@
         out_shape=(
             shape,
             jax.ShapeDtypeStruct((8, 128, 256), F32),
-            jax.ShapeDtypeStruct((8, 128, 256), BF16),
+            jax.ShapeDtypeStruct((8, 128, 256), F32),
             jax.ShapeDtypeStruct((2048, 128), F32),
-            jax.ShapeDtypeStruct((128, 128), BF16),
             jax.ShapeDtypeStruct((128, 128), BF16),
             jax.ShapeDtypeStruct((128, 256), F32),
         ),
         in_specs=[hbm] * 6,
-        out_specs=(vmem,) * 7,
+        out_specs=(vmem,) * 6,
         scratch_shapes=[
             pltpu.VMEM((32, 64, 128), BF16),
             pltpu.VMEM((2, 128, 512), BF16),
@@ -367,6 +424,7 @@
             pltpu.VMEM((2, 128, 128), BF16),
             pltpu.VMEM((2, 128, 128), BF16),
             pltpu.VMEM((2, 2, 128, 256), F32),
+            pltpu.VMEM((8, 128, 256), BF16),
             pltpu.VMEM((2048, 128), F32),
             pltpu.VMEM((2048, 128), F32),
             tiles,
@@ -379,6 +437,8 @@
             tiles,
             tiles,
             dma((6,)),
+            dma((2,)),
+            dma((2, 4)),
             dma((2,)),
             dma((2,)),
             dma((2, 4)),
@@ -392,7 +452,7 @@
     return pl.pallas_call(
         last_kernel,
         out_shape=(shape, shape),
-        in_specs=[vmem] * 7,
+        in_specs=[vmem] * 6,
         out_specs=(hbm, hbm),
         scratch_shapes=[pltpu.VMEM((32, 64, 128), BF16), dma, dma],
         compiler_params=pltpu.CompilerParams(vmem_limit_bytes=16 << 20),

time: 61.6 us -> 60.4 us (0.981)
  Pallas kernels: 60.9 us -> 59.7 us
    pallas_call x1, Pallas kernels: 59.1 us -> 57.9 us  [local(): pl.pallas_call(kernel, out_shape=(shape, jax.ShapeDtypeStruct((8, 128, 25...]
where the time goes in v5:
time: 60.4 us; the launch traced here: 60.3 us
  Pallas kernels  59.7 us (99%)
  between operations  0.64 us (1%)
    pallas_call x1, Pallas kernels, local(): pl.pallas_call(kernel, out_shape=(shape, jax.ShapeDtypeStruct((8, 128, 25...  57.9 us
    pallas_call x1, Pallas kernels, local(): pl.pallas_call(last_kernel, out_shape=(shape, shape), in_specs=[vmem] * 6...  1.72 us

profile of v5, /device:TPU:1, one launch (start us, length us, event | category | flops | bytes accessed | tf_op | source)
XLA Modules:
  0.0 60.3 jit_solution(11687822335042636805)
XLA Ops:
  0.6 57.9 %triangle.1 = (bf16[32,64,128]{2,1,0:T(8,128)(2,1)S(1)}, f32[8,128,256]{2,1,0:T(8,128)S(1)}, f32[8,128,256]{2,1,0:T(8,128)S(1)}, f32[2048,128]{1,0:T(8,128)S(1)}...) custom-call(bf16[32,64,128]{2,1,0:T(8,128)(2,1)} %pair_hbm.1, f32[2,128]{1,0:T(2,128)} %in_gain_hbm.1, ...), custom_call_target="tpu_custom_call" | custom-call | tf_op jit(solution)/shard_map/triangle/pallas_call | solution.py:404
  58.6 1.7 %last.1 = (bf16[32,64,128]{2,1,0:T(8,128)(2,1)}, bf16[32,64,128]{2,1,0:T(8,128)(2,1)}) custom-call(bf16[32,64,128]{2,1,0:T(8,128)(2,1)S(1)} %get-tuple-element.8.first, f32[8,128,256]{2,1,0:T(8,128)S(1)} %get-tuple-element.9.zt, f32[8,128,256]{2,1,0:T(8,128)S(1)} %get-tuple-element.10.gate, f32[2048,128]{1,0:T(8,128)S(1)} %get-tuple-element.11.flat_t, ...), custom_call_target="tpu_custom_call" | custom-call | tf_op jit(solution)/shard_map/last/pallas_call | solution.py:452

commit v6 on v5

--- a/solution.py
+++ b/solution.py
@@ -9,7 +9,6 @@
 MESH = pl.DeviceIdType.MESH
 F32 = jnp.float32
 BF16 = jnp.bfloat16
-UNROLL = 8
 FARTHEST = 0x3124756
 GROUPS = (((2, 1), (2, 0)), ((1, 1), (3, 0)), ((3, 1), (1, 0)), ((0, 1), (0, 0)))
 NT = (((1,), (1,)), ((), ()))
@@ -133,7 +132,7 @@
 
             return carry
 
-        lax.fori_loop(0, 8, step, 0, unroll=UNROLL)
+        lax.fori_loop(0, 8, step, 0, unroll=8)
 
     def shifted(zs, lo, g):
         return [(mod4(zs + dz), jnp.bitwise_xor(lo, dl)) for dz, dl in GROUPS[g]]
@@ -199,7 +198,7 @@
     lax.fori_loop(0, 8, first, 0, unroll=4)
     pl.semaphore_wait(barrier, 127)
 
-    def send_side(u, flat, send, recv, out_sem, in_sem, group, skip_self):
+    def send_side(u, flat, send, recv, out_sem, in_sem, group, skip_self, core):
         def one(tr, tc):
             d = tr * 8 + tc
             send[u, d] = flat[pl.ds(pl.multiple_of(d * 16, 16), 16), :].astype(BF16)
@@ -212,7 +211,7 @@
                 device_id_type=MESH,
             ).start()
 
-        visit(group, skip_self, one)
+        visit(group, skip_self, one, core)
 
     def wait_tiles(ref, sem, count):
         pltpu.make_async_copy(ref.at[pl.ds(0, count)], ref.at[pl.ds(0, count)], sem).wait()
@@ -244,7 +243,7 @@
     def sent_right(u):
         wait_tiles(send_r.at[u], send_r_sem.at[u], 127)
 
-    for u in range(2):
+    def send_right(u, core):
         for g in range(4):
             send_side(
                 u,
@@ -255,14 +254,10 @@
                 recv_r_sem.at[u],
                 shifted(z, x_lo, g),
                 has_own(g),
+                core,
             )
-        own(u, flat_r, recv_r)
-
-        def late_left(q, carry):
-            project(u, q, 0, flat_l)
-            return carry
-
-        lax.fori_loop(0, 8, late_left, 0, unroll=4)
+
+    def send_left(u, core):
         for g in range(4):
             send_side(
                 u,
@@ -273,7 +268,21 @@
                 recv_l_sem.at[u, g],
                 shifted(*left_base(u), g),
                 u == 1 or has_own(g),
+                core,
             )
+
+    for u in range(2):
+
+        def late_left(q, carry):
+            project(u, q, 0, flat_l)
+            return carry
+
+        send_right(u, 0)
+        lax.fori_loop(0, 8, late_left, 0, unroll=4)
+        send_left(u, 0)
+        send_right(u, 1)
+        send_left(u, 1)
+        own(u, flat_r, recv_r)
         own(u, flat_l, recv_l)
         if u == 0:
             for load in loads[3:]:
@@ -357,10 +366,7 @@
                     tsend[u, at] = lo
                     tsend[u, at + 1] = hi
 
-            visit(group, has_own(g), home, 0 if u == 0 else None)
-        if u == 0:
-            for g in range(4):
-                visit(back(g), has_own(g), home, 1)
+            visit(group, has_own(g), home)
         trecv[u, mine] = tsend[u, mine]
         wait_tiles(trecv.at[u], recv_t_sem.at[u], 127)
 

time: 60.4 us -> 58.3 us (0.965)
  Pallas kernels: 59.7 us -> 57.6 us
    pallas_call x1, Pallas kernels: 57.9 us -> 55.9 us  [local(): pl.pallas_call(kernel, out_shape=(shape, jax.ShapeDtypeStruct((8, 128, 25...]
where the time goes in v6:
time: 58.3 us; the launch traced here: 58.2 us
  Pallas kernels  57.6 us (99%)
  between operations  0.64 us (1%)
    pallas_call x1, Pallas kernels, local(): pl.pallas_call(kernel, out_shape=(shape, jax.ShapeDtypeStruct((8, 128, 25...  55.9 us
    pallas_call x1, Pallas kernels, local(): pl.pallas_call(last_kernel, out_shape=(shape, shape), in_specs=[vmem] * 6...  1.72 us

profile of v6, /device:TPU:1, one launch (start us, length us, event | category | flops | bytes accessed | tf_op | source)
XLA Modules:
  0.0 58.2 jit_solution(10758513879105315109)
XLA Ops:
  0.6 55.9 %triangle.1 = (bf16[32,64,128]{2,1,0:T(8,128)(2,1)S(1)}, f32[8,128,256]{2,1,0:T(8,128)S(1)}, f32[8,128,256]{2,1,0:T(8,128)S(1)}, f32[2048,128]{1,0:T(8,128)S(1)}...) custom-call(bf16[32,64,128]{2,1,0:T(8,128)(2,1)} %pair_hbm.1, f32[2,128]{1,0:T(2,128)} %in_gain_hbm.1, ...), custom_call_target="tpu_custom_call" | custom-call | tf_op jit(solution)/shard_map/triangle/pallas_call | solution.py:410
  56.5 1.7 %last.1 = (bf16[32,64,128]{2,1,0:T(8,128)(2,1)}, bf16[32,64,128]{2,1,0:T(8,128)(2,1)}) custom-call(bf16[32,64,128]{2,1,0:T(8,128)(2,1)S(1)} %get-tuple-element.8.first, f32[8,128,256]{2,1,0:T(8,128)S(1)} %get-tuple-element.9.zt, f32[8,128,256]{2,1,0:T(8,128)S(1)} %get-tuple-element.10.gate, f32[2048,128]{1,0:T(8,128)S(1)} %get-tuple-element.11.flat_t, ...), custom_call_target="tpu_custom_call" | custom-call | tf_op jit(solution)/shard_map/last/pallas_call | solution.py:458

commit v7 on v6

--- a/solution.py
+++ b/solution.py
@@ -388,7 +388,7 @@
                 project(1, q, 1, flat_r)
                 return carry
 
-            lax.fori_loop(0, 8, finish, 0, unroll=4)
+            lax.fori_loop(0, 8, finish, 0, unroll=8)
 
     for u in range(2):
         sent_right(u)

time: 58.3 us -> 58 us (level)
  no operation moved by 1% of the time
where the time goes in v7:
time: 58 us; the launch traced here: 57.9 us
  Pallas kernels  57.3 us (99%)
  between operations  0.64 us (1%)
    pallas_call x1, Pallas kernels, local(): pl.pallas_call(kernel, out_shape=(shape, jax.ShapeDtypeStruct((8, 128, 25...  55.6 us
    pallas_call x1, Pallas kernels, local(): pl.pallas_call(last_kernel, out_shape=(shape, shape), in_specs=[vmem] * 6...  1.72 us

profile of v7, /device:TPU:1, one launch (start us, length us, event | category | flops | bytes accessed | tf_op | source)
XLA Modules:
  0.0 57.9 jit_solution(3588600315054242501)
XLA Ops:
  0.6 55.6 %triangle.1 = (bf16[32,64,128]{2,1,0:T(8,128)(2,1)S(1)}, f32[8,128,256]{2,1,0:T(8,128)S(1)}, f32[8,128,256]{2,1,0:T(8,128)S(1)}, f32[2048,128]{1,0:T(8,128)S(1)}...) custom-call(bf16[32,64,128]{2,1,0:T(8,128)(2,1)} %pair_hbm.1, f32[2,128]{1,0:T(2,128)} %in_gain_hbm.1, ...), custom_call_target="tpu_custom_call" | custom-call | tf_op jit(solution)/shard_map/triangle/pallas_call | solution.py:410
  56.2 1.7 %last.1 = (bf16[32,64,128]{2,1,0:T(8,128)(2,1)}, bf16[32,64,128]{2,1,0:T(8,128)(2,1)}) custom-call(bf16[32,64,128]{2,1,0:T(8,128)(2,1)S(1)} %get-tuple-element.8.first, f32[8,128,256]{2,1,0:T(8,128)S(1)} %get-tuple-element.9.zt, f32[8,128,256]{2,1,0:T(8,128)S(1)} %get-tuple-element.10.gate, f32[2048,128]{1,0:T(8,128)S(1)} %get-tuple-element.11.flat_t, ...), custom_call_target="tpu_custom_call" | custom-call | tf_op jit(solution)/shard_map/last/pallas_call | solution.py:458

commit v8 on v7

--- a/solution.py
+++ b/solution.py
@@ -6,6 +6,7 @@
 from jax.sharding import PartitionSpec as P
 
 EPS = 1e-05
+FLAT = 128 * 16 + 16
 MESH = pl.DeviceIdType.MESH
 F32 = jnp.float32
 BF16 = jnp.bfloat16
@@ -413,7 +414,7 @@
             shape,
             jax.ShapeDtypeStruct((8, 128, 256), F32),
             jax.ShapeDtypeStruct((8, 128, 256), F32),
-            jax.ShapeDtypeStruct((2048, 128), F32),
+            jax.ShapeDtypeStruct((FLAT, 128), F32),
             jax.ShapeDtypeStruct((128, 128), BF16),
             jax.ShapeDtypeStruct((128, 256), F32),
         ),
@@ -431,8 +432,8 @@
             pltpu.VMEM((2, 128, 128), BF16),
             pltpu.VMEM((2, 2, 128, 256), F32),
             pltpu.VMEM((8, 128, 256), BF16),
-            pltpu.VMEM((2048, 128), F32),
-            pltpu.VMEM((2048, 128), F32),
+            pltpu.VMEM((FLAT, 128), F32),
+            pltpu.VMEM((FLAT, 128), F32),
             tiles,
             tiles,
             tiles,

time: 58 us -> 58.1 us (level)
  no operation moved by 1% of the time
where the time goes in v8:
time: 58.1 us; the launch traced here: 58 us
  Pallas kernels  57.3 us (99%)
  between operations  0.64 us (1%)
    pallas_call x1, Pallas kernels, local(): pl.pallas_call(kernel, out_shape=(shape, jax.ShapeDtypeStruct((8, 128, 25...  55.6 us
    pallas_call x1, Pallas kernels, local(): pl.pallas_call(last_kernel, out_shape=(shape, shape), in_specs=[vmem] * 6...  1.76 us

profile of v8, /device:TPU:1, one launch (start us, length us, event | category | flops | bytes accessed | tf_op | source)
XLA Modules:
  0.0 58.0 jit_solution(16720065299313235193)
XLA Ops:
  0.6 55.6 %triangle.1 = (bf16[32,64,128]{2,1,0:T(8,128)(2,1)S(1)}, f32[8,128,256]{2,1,0:T(8,128)S(1)}, f32[8,128,256]{2,1,0:T(8,128)S(1)}, f32[2064,128]{1,0:T(8,128)S(1)}...) custom-call(bf16[32,64,128]{2,1,0:T(8,128)(2,1)} %pair_hbm.1, f32[2,128]{1,0:T(2,128)} %in_gain_hbm.1, ...), custom_call_target="tpu_custom_call" | custom-call | tf_op jit(solution)/shard_map/triangle/pallas_call | solution.py:411
  56.2 1.8 %last.1 = (bf16[32,64,128]{2,1,0:T(8,128)(2,1)}, bf16[32,64,128]{2,1,0:T(8,128)(2,1)}) custom-call(bf16[32,64,128]{2,1,0:T(8,128)(2,1)S(1)} %get-tuple-element.8.first, f32[8,128,256]{2,1,0:T(8,128)S(1)} %get-tuple-element.9.zt, f32[8,128,256]{2,1,0:T(8,128)S(1)} %get-tuple-element.10.gate, f32[2064,128]{1,0:T(8,128)S(1)} %get-tuple-element.11.flat_t, ...), custom_call_target="tpu_custom_call" | custom-call | tf_op jit(solution)/shard_map/last/pallas_call | solution.py:459
